TPU v7x, 256 devices: a whole 4x4x8 slice. The times are simulated.
256 devices in a mesh: row: 16 (over y_lo, x, core), col: 16 (over y_hi, z).
Axes of the slice: x: 4, y: 4 (y_hi: 2, y_lo: 2; y = y_hi * 2 + y_lo), z: 8, core: 2. Of those that a mesh axis runs over, the one named last changes fastest.
Arguments:
- places: float32 [256, 4, 256], P(('row', 'col')), may hold values from 0 to 8, as said below
- omega: bfloat16 [256, 64, 256], P(('row', 'col')), may hold values from -6 to 6
- pairs: int32 [32768, 2], P(('row', 'col')), may hold values from -1 to 255, as said below
Outputs:
- bases: float32 [256, 64, 256], P(('row', 'col'))
- coeffs: bfloat16 [32768, 64, 256], P(('row', 'col'))
Inputs may be any that keep to these rules, and one draw needn't show every extreme that they name: Device d (in row+col order, grid row d // 16 = a, grid column d % 16 = b) holds slots d * 128 to (d + 1) * 128 - 1. Its live slots come first and hold distinct pairs (t, s) with t % 16 = b and s // (1 * 16) = a; the rest hold -1 in both columns. Every block is the target of a live slot on each device whose target set contains it. Each device has at least 32 and at most 128 live slots, and some device has all 128. `places`: rows 0 to 2 are coordinates, row 3 holds weights of 0.25 or more.
All inputs are finite; a program needn't handle non-finite values.
Results may differ from a plain program's by a relative error of at most 0.0027.
The roundings to bfloat16 on the way count: a program that leaves them out, or rounds other values in their place, can miss the bound.
Values may be sent and summed in bfloat16 or wider, within the bound.
A program may use at most 64 MiB of HBM per device.

v0:
```python
import math

import jax
import jax.numpy as jnp
from jax import lax
from jax.sharding import PartitionSpec as P

soft_sq = 0.09
ridge = 0.05


def kernel_tile(target_spots, source_spots):
    dist_sq = (target_spots[..., 0, :, None] - source_spots[..., 0, None, :]) ** 2
    dist_sq = dist_sq + (target_spots[..., 1, :, None] - source_spots[..., 1, None, :]) ** 2
    dist_sq = dist_sq + (target_spots[..., 2, :, None] - source_spots[..., 2, None, :]) ** 2
    return (source_spots[..., 3, None, :] * lax.rsqrt(dist_sq + soft_sq)).astype(jnp.bfloat16)


def factor(sketch):
    gram = jnp.einsum("tri,tsi->trs", sketch, sketch, precision=lax.Precision.HIGHEST)
    energy = jnp.sum(sketch * sketch, axis=(1, 2))
    shift = ridge * energy / sketch.shape[1]
    gram = gram + shift[:, None, None] * jnp.eye(sketch.shape[1], dtype=sketch.dtype)[None, :, :]
    lower = jnp.linalg.cholesky(gram)
    return lax.linalg.triangular_solve(lower, sketch, left_side=True, lower=True)


def body(places, omega, pairs):
    col_count = lax.axis_size("col")
    row_at = lax.axis_index("row")
    per_device = places.shape[0]
    panel_count = places.shape[2]
    rank_count = omega.shape[1]
    slot_count = pairs.shape[0]
    batch_slots = min(16, slot_count)
    tgt_places = lax.all_gather(places, "row", axis=0, tiled=True)
    src_places = lax.all_gather(places, "col", axis=0, tiled=True)
    tgt_count = tgt_places.shape[0]
    alive = pairs[:, 0] >= 0
    pair_tgt = jnp.where(alive, pairs[:, 0], 0)
    pair_src = jnp.where(alive, pairs[:, 1], 0)
    tgt_local = jnp.where(
        alive, pair_tgt // per_device // col_count * per_device + pair_tgt % per_device, 0
    )
    src_local = jnp.where(alive, pair_src - row_at * col_count * per_device, 0)
    alive_float = alive.astype(jnp.float32)
    live_count = jnp.sum(alive.astype(jnp.int32))
    turns = (live_count + batch_slots - 1) // batch_slots
    empty = jnp.zeros((tgt_count, rank_count, panel_count), jnp.float32)
    target_range = jnp.arange(tgt_count, dtype=jnp.int32)
    piece = lax.all_gather(omega, "col", axis=0, tiled=True)

    def one_source(member, running):
        panel = lax.dynamic_index_in_dim(piece, member, 0, keepdims=False)
        spot = lax.dynamic_index_in_dim(src_places, member, 0, keepdims=True)
        hits = (
            (tgt_local[None, :] == target_range[:, None])
            & (src_local[None, :] == member)
            & alive[None, :]
        )
        weight = jnp.sum(hits.astype(jnp.float32), axis=1)
        kernel = kernel_tile(tgt_places, spot)
        contrib = jnp.einsum("rj,tij->tri", panel, kernel, preferred_element_type=jnp.float32)
        return running + weight[:, None, None] * contrib

    partial_sketch = lax.fori_loop(0, piece.shape[0], one_source, empty)
    own_sketch = lax.psum_scatter(partial_sketch, "row", scatter_dimension=0, tiled=True)
    own_basis = factor(own_sketch)
    bases = own_basis * math.sqrt(panel_count)
    basis_all = lax.all_gather(own_basis.astype(jnp.bfloat16), "row", axis=0, tiled=True)

    def projection_update(turn, buffer):
        first = turn * batch_slots
        tgt_group = lax.dynamic_slice_in_dim(tgt_local, first, batch_slots)
        src_group = lax.dynamic_slice_in_dim(src_local, first, batch_slots)
        live_group = lax.dynamic_slice_in_dim(alive_float, first, batch_slots)
        kernel = kernel_tile(
            jnp.take(tgt_places, tgt_group, axis=0), jnp.take(src_places, src_group, axis=0)
        )
        result = jnp.einsum(
            "pri,pij->prj",
            jnp.take(basis_all, tgt_group, axis=0),
            kernel,
            preferred_element_type=jnp.float32,
        )
        result = (result * live_group[:, None, None]).astype(jnp.bfloat16)
        return lax.dynamic_update_slice_in_dim(buffer, result, first, 0)

    coeffs = lax.fori_loop(
        0, turns, projection_update, jnp.zeros((slot_count, rank_count, panel_count), jnp.bfloat16)
    )
    return (bases, coeffs)


def solution(mesh):
    in_specs = (
        P(("row", "col"), None, None),
        P(("row", "col"), None, None),
        P(("row", "col"), None),
    )
    out_specs = (P(("row", "col"), None, None), P(("row", "col"), None, None))
    return jax.shard_map(body, mesh=mesh, in_specs=in_specs, out_specs=out_specs, check_vma=False)
```

profile of v0, /device:TPU:1, one launch (start us, length us, event | category | flops | bytes accessed | tf_op | source)
XLA Modules:
  0.0 291.7 jit_solution(7763276547528916221)
XLA Ops:
  7.2 21.4 %all_gather.13 = f32[16,4,256]{2,1,0:T(4,128)S(1)} all-gather(f32[1,4,256]{2,1,0:T(4,128)} %param.9), channel_id=1, replica_groups=mesh['row'=16,'col'=16] {'row'}, dimensions={0}, use_global_device_ids=true | all-gather | bytes 69632 | tf_op jit(solution)/shard_map/all_gather | solution.py:36
  28.7 37.0 %all_gather.12 = f32[16,4,256]{2,1,0:T(4,128)S(1)} all-gather(f32[1,4,256]{2,1,0:T(4,128)} %param.9), channel_id=1, replica_groups=mesh['row'=16,'col'=16] {'col'}, dimensions={0}, use_global_device_ids=true | all-gather | bytes 69632 | tf_op jit(solution)/shard_map/all_gather | solution.py:37
  65.7 0.7 fusion.38
  66.4 1.4 convert_reduce_fusion.1
  67.8 32.6 %all_gather.14 = bf16[16,64,256]{2,1,0:T(8,128)(2,1)S(1)} all-gather(bf16[1,64,256]{2,1,0:T(8,128)(2,1)} %param.10), channel_id=1, replica_groups=mesh['row'=16,'col'=16] {'col'}, dimensions={0}, use_global_device_ids=true | all-gather | bytes 557056 | tf_op jit(solution)/shard_map/all_gather | solution.py:51
  100.4 36.1 %while.25 = (s32[]{:T(128)}, f32[16,64,256]{2,1,0:T(8,128)S(1)}, s32[128]{0:T(128)S(1)}, s32[128]{0:T(128)S(1)}, pred[128]{0:T(512)(128)(4,1)S(1)}, /*index=5*/f...) while((s32[]{:T(128)}, f32[16,64,256]{2,1,0:T(8,128)S(1)}, ...), condition=%wide.region_2.3_spmd.clone, body=%wide.region_0.2_spmd.clone.sunk | while | flops 146548848 | bytes 2291851 | solution.py:66
  100.4 0.1 convert_reduce_fusion.3
  100.5 2.1 fusion.57
  102.8 2.1 fusion.57
  105.0 2.1 fusion.57
  107.3 2.1 fusion.57
  109.6 2.1 fusion.57
  111.8 2.1 fusion.57
  113.9 0.1 convert_reduce_fusion.3
  114.1 2.1 fusion.57
  116.3 2.1 fusion.57
  118.6 2.1 fusion.57
  120.8 2.1 fusion.57
  123.1 2.1 fusion.57
  125.4 2.1 fusion.57
  127.6 2.1 fusion.57
  129.9 2.1 fusion.57
  132.1 2.1 fusion.57
  134.4 2.1 fusion.57
  136.5 1.0 copy-done
  138.1 66.1 %reduce-scatter.2.cloned.1.call-done = f32[1,64,256]{2,1,0:T(8,128)} async-done(((f32[16,64,256]{2,1,0:T(8,128)}), f32[1,64,256]{2,1,0:T(8,128)}) %reduce-scatter.2.cloned.1.call-update) | async-done | bytes 65552 | tf_op jit(solution)/shard_map/reduce_scatter | solution.py:67
  204.2 1.5 multiply_reduce_fusion
  206.3 1.1 convolution_add_fusion
  207.5 5.8 %custom-call.7 = f32[1,64,64]{2,1,0:T(8,128)S(1)} custom-call(f32[1,64,64]{2,1,0:T(8,128)S(1)} %fusion.33), custom_call_target="Cholesky" | custom-call | tf_op jit(solution)/shard_map/jit(cholesky)/cholesky | solution.py:24
  213.4 0.6 compare_reduce_fusion
  214.1 0.7 fusion.32
  214.7 4.9 %custom-call.8 = f32[1,1,64,64]{2,3,1,0:T(8,128)S(1)} custom-call(f32[1,1,64,64]{3,2,1,0:T(8,128)S(1)} %fusion.32), custom_call_target="InvertDiagBlocksLowerTriangular" | custom-call | tf_op jit(solution)/shard_map/triangular_solve | solution.py:25
  219.6 1.7 fusion.41
  221.4 21.4 %all-gather = bf16[1024,256]{1,0:T(8,128)(2,1)S(1)} all-gather(bf16[64,256]{1,0:T(8,128)(2,1)S(1)} %get-tuple-element.315), channel_id=2, replica_groups=mesh['row'=16,'col'=16] {'row'}, dimensions={0}, use_global_device_ids=true | all-gather | bytes 557056 | tf_op jit(solution)/shard_map/all_gather | solution.py:70
  242.8 2.5 broadcast_in_dim.55
  245.3 39.6 %while.24 = (s32[]{:T(128)}, bf16[128,64,256]{2,1,0:T(8,128)(2,1)}, s32[]{:T(128)}, s32[128]{0:T(128)S(1)}, bf16[16,64,256]{2,1,0:T(8,128)(2,1)S(1)}, /*index=5*...) while((s32[]{:T(128)}, bf16[128,64,256]{2,1,0:T(8,128)(2,1)}, ...), condition=%wide.region_9.11_spmd, body=%wide.region_8.10_spmd.sunk | while | flops 146573504 | bytes 3204103 | solution.py:89
  245.5 0.6 gather_fusion
  246.3 0.6 gather_fusion.1
  247.1 0.6 gather_fusion.2
  247.7 3.3 %fusion.55 = bf16[128,64,256]{2,1,0:T(8,128)(2,1)} fusion(bf16[128,64,256]{2,1,0:T(8,128)(2,1)} %get-tuple-element.516, s32[]{:T(128)S(6)} %select_n.106, f32[16,256]{1,0:T(8,128)S(1)} %bitcast.110, f32[16,256]{1,0:T(8,128)S(1)} %bitcast.114, f32[16,256]{1,0:T(8,128)S(1)} %bitcast.111, f32[16,256]{1,0:T(8,128)S(1)} %bitcast.115, ...), kind=kOutput, calls=%fused_computation.37.clone.1 | convolution fusion | flops 146538496 | bytes 1163348 | tf_op jit(solution)/shard_map/while/body/pri,pij->prj/dot_general | solution.py:80
  251.2 0.6 gather_fusion
  252.0 0.6 gather_fusion.1
  252.7 0.6 gather_fusion.2
  253.3 3.3 %fusion.55 = bf16[128,64,256]{2,1,0:T(8,128)(2,1)} fusion(bf16[128,64,256]{2,1,0:T(8,128)(2,1)} %get-tuple-element.516, s32[]{:T(128)S(6)} %select_n.106, f32[16,256]{1,0:T(8,128)S(1)} %bitcast.110, f32[16,256]{1,0:T(8,128)S(1)} %bitcast.114, f32[16,256]{1,0:T(8,128)S(1)} %bitcast.111, f32[16,256]{1,0:T(8,128)S(1)} %bitcast.115, ...), kind=kOutput, calls=%fused_computation.37.clone.1 | convolution fusion | flops 146538496 | bytes 1163348 | tf_op jit(solution)/shard_map/while/body/pri,pij->prj/dot_general | solution.py:80
  256.8 0.6 gather_fusion
  257.6 0.6 gather_fusion.1
  258.4 0.6 gather_fusion.2
  259.0 3.3 %fusion.55 = bf16[128,64,256]{2,1,0:T(8,128)(2,1)} fusion(bf16[128,64,256]{2,1,0:T(8,128)(2,1)} %get-tuple-element.516, s32[]{:T(128)S(6)} %select_n.106, f32[16,256]{1,0:T(8,128)S(1)} %bitcast.110, f32[16,256]{1,0:T(8,128)S(1)} %bitcast.114, f32[16,256]{1,0:T(8,128)S(1)} %bitcast.111, f32[16,256]{1,0:T(8,128)S(1)} %bitcast.115, ...), kind=kOutput, calls=%fused_computation.37.clone.1 | convolution fusion | flops 146538496 | bytes 1163348 | tf_op jit(solution)/shard_map/while/body/pri,pij->prj/dot_general | solution.py:80
  262.5 0.6 gather_fusion
  263.3 0.6 gather_fusion.1
  264.0 0.6 gather_fusion.2
  264.6 3.3 %fusion.55 = bf16[128,64,256]{2,1,0:T(8,128)(2,1)} fusion(bf16[128,64,256]{2,1,0:T(8,128)(2,1)} %get-tuple-element.516, s32[]{:T(128)S(6)} %select_n.106, f32[16,256]{1,0:T(8,128)S(1)} %bitcast.110, f32[16,256]{1,0:T(8,128)S(1)} %bitcast.114, f32[16,256]{1,0:T(8,128)S(1)} %bitcast.111, f32[16,256]{1,0:T(8,128)S(1)} %bitcast.115, ...), kind=kOutput, calls=%fused_computation.37.clone.1 | convolution fusion | flops 146538496 | bytes 1163348 | tf_op jit(solution)/shard_map/while/body/pri,pij->prj/dot_general | solution.py:80
  268.1 0.6 gather_fusion
  268.9 0.6 gather_fusion.1
  269.7 0.6 gather_fusion.2
  270.3 3.3 %fusion.55 = bf16[128,64,256]{2,1,0:T(8,128)(2,1)} fusion(bf16[128,64,256]{2,1,0:T(8,128)(2,1)} %get-tuple-element.516, s32[]{:T(128)S(6)} %select_n.106, f32[16,256]{1,0:T(8,128)S(1)} %bitcast.110, f32[16,256]{1,0:T(8,128)S(1)} %bitcast.114, f32[16,256]{1,0:T(8,128)S(1)} %bitcast.111, f32[16,256]{1,0:T(8,128)S(1)} %bitcast.115, ...), kind=kOutput, calls=%fused_computation.37.clone.1 | convolution fusion | flops 146538496 | bytes 1163348 | tf_op jit(solution)/shard_map/while/body/pri,pij->prj/dot_general | solution.py:80
  273.8 0.6 gather_fusion
  274.6 0.6 gather_fusion.1
  275.3 0.6 gather_fusion.2
  275.9 3.3 %fusion.55 = bf16[128,64,256]{2,1,0:T(8,128)(2,1)} fusion(bf16[128,64,256]{2,1,0:T(8,128)(2,1)} %get-tuple-element.516, s32[]{:T(128)S(6)} %select_n.106, f32[16,256]{1,0:T(8,128)S(1)} %bitcast.110, f32[16,256]{1,0:T(8,128)S(1)} %bitcast.114, f32[16,256]{1,0:T(8,128)S(1)} %bitcast.111, f32[16,256]{1,0:T(8,128)S(1)} %bitcast.115, ...), kind=kOutput, calls=%fused_computation.37.clone.1 | convolution fusion | flops 146538496 | bytes 1163348 | tf_op jit(solution)/shard_map/while/body/pri,pij->prj/dot_general | solution.py:80
  279.4 0.6 gather_fusion
  280.2 0.6 gather_fusion.1
  281.0 0.6 gather_fusion.2
  281.6 3.3 %fusion.55 = bf16[128,64,256]{2,1,0:T(8,128)(2,1)} fusion(bf16[128,64,256]{2,1,0:T(8,128)(2,1)} %get-tuple-element.516, s32[]{:T(128)S(6)} %select_n.106, f32[16,256]{1,0:T(8,128)S(1)} %bitcast.110, f32[16,256]{1,0:T(8,128)S(1)} %bitcast.114, f32[16,256]{1,0:T(8,128)S(1)} %bitcast.111, f32[16,256]{1,0:T(8,128)S(1)} %bitcast.115, ...), kind=kOutput, calls=%fused_computation.37.clone.1 | convolution fusion | flops 146538496 | bytes 1163348 | tf_op jit(solution)/shard_map/while/body/pri,pij->prj/dot_general | solution.py:80
  (175 shorter events, 5.3 us)
Async XLA Ops:
  7.2 197.0 %reduce-scatter.2.cloned.1.call-start = ((), (), s32[]{:S(2)}) async-start(), calls=%async_computation.1 | async-start | bytes 1114112 | tf_op jit(solution)/shard_map/reduce_scatter | solution.py:67
  136.5 1.0 copy-start
Sparse Core Ops, SparseCore 0:
  137.6 66.5 reduce-scatter.1
where the time goes:
time: 297 us; the launch traced here: 292 us
  blocking collectives  112 us (38%)
  waiting for transfers between devices  66.1 us (22%)
  matrix products  59.3 us (20%)
  other arithmetic  19.4 us (7%)
  local copies, waits for them, and re-layouts  17.5 us (6%)
  between operations  15.4 us (5%)
    reduce_scatter x1, waiting for transfers between devices, body(): lax.psum_scatter(partial_sketch, 'row', scatter_dimension=0, tiled=True)  66.1 us
    all_gather x1, blocking collectives, body(): src_places = lax.all_gather(places, 'col', axis=0, tiled=True)  37 us
    dot_general x16, matrix products, one_source(): jnp.einsum('rj,tij->tri', panel, kernel, preferred_element_type=jnp.float32)  33.1 us
    all_gather x1, blocking collectives, body(): piece = lax.all_gather(omega, 'col', axis=0, tiled=True)  32.6 us
    dot_general x7, matrix products, projection_update(): jnp.einsum('pri,pij->prj', jnp.take(basis_all, tgt_group, axis=0), kernel...  23.3 us
    all_gather x1, blocking collectives, body(): tgt_places = lax.all_gather(places, 'row', axis=0, tiled=True)  21.4 us
    all_gather x1, blocking collectives, body(): lax.all_gather(own_basis.astype(jnp.bfloat16), 'row', axis=0, tiled=True)  21.4 us
    another operation x3, other arithmetic, factor(): lower = jnp.linalg.cholesky(gram)  6.52 us
  transfers between devices with their start and end apart: 1, of which 1 were waited for; matrix products, arithmetic and copies ran while one was open for 0% of the time, Pallas kernels for 0%

commit v1 on v0

v1 whole, which is shorter than its diff:
```python
import functools
import math

import jax
import jax.numpy as jnp
from jax import lax
from jax.experimental import pallas as pl
from jax.experimental.pallas import tpu as pltpu
from jax.sharding import PartitionSpec as P

soft_sq = 0.09
ridge = 0.05
MESH = pl.DeviceIdType.MESH
VMEM = pltpu.VMEM
GROUP = 4


def gather_kernel(rows, cols, places_ref, omega_ref, tgt_ref, src_ref, omegas_ref,
                  own_sem, row_send, row_recv, col_send, col_recv, om_send, om_recv):
    row, col = lax.axis_index("row"), lax.axis_index("col")
    barrier = pltpu.get_barrier_semaphore()
    for k in range(1, cols):
        pl.semaphore_signal(barrier, inc=1, device_id=(row, lax.rem(col + k, cols)), device_id_type=MESH)
    for k in range(1, rows):
        pl.semaphore_signal(barrier, inc=1, device_id=(lax.rem(row + k, rows), col), device_id_type=MESH)
    own = [
        pltpu.make_async_copy(places_ref, tgt_ref.at[pl.ds(row, 1)], own_sem.at[0]),
        pltpu.make_async_copy(places_ref, src_ref.at[pl.ds(col, 1)], own_sem.at[1]),
        pltpu.make_async_copy(omega_ref, omegas_ref.at[pl.ds(col, 1)], own_sem.at[2]),
    ]
    for c in own:
        c.start()
    pl.semaphore_wait(barrier, rows + cols - 2)

    def row_copy(k, slot):
        return pltpu.make_async_remote_copy(
            src_ref=places_ref, dst_ref=tgt_ref.at[pl.ds(slot, 1)], send_sem=row_send.at[k],
            recv_sem=row_recv.at[k], device_id=(lax.rem(row + k, rows), col), device_id_type=MESH)

    def col_copy(k, slot):
        return pltpu.make_async_remote_copy(
            src_ref=places_ref, dst_ref=src_ref.at[pl.ds(slot, 1)], send_sem=col_send.at[k],
            recv_sem=col_recv.at[k], device_id=(row, lax.rem(col + k, cols)), device_id_type=MESH)

    def om_copy(k, slot):
        return pltpu.make_async_remote_copy(
            src_ref=omega_ref, dst_ref=omegas_ref.at[pl.ds(slot, 1)], send_sem=om_send.at[k],
            recv_sem=om_recv.at[k], device_id=(row, lax.rem(col + k, cols)), device_id_type=MESH)

    for k in range(1, cols):
        col_copy(k, col).start()
    for k in range(1, rows):
        row_copy(k, row).start()
    for k in range(1, cols):
        om_copy(k, col).start()
    for c in own:
        c.wait()
    for k in range(1, cols):
        col_copy(k, lax.rem(col + cols - k, cols)).wait()
        om_copy(k, lax.rem(col + cols - k, cols)).wait()
    for k in range(1, rows):
        row_copy(k, lax.rem(row + rows - k, rows)).wait()


def gather_all(places, omega, rows, cols):
    return pl.pallas_call(
        functools.partial(gather_kernel, rows, cols),
        out_shape=[
            jax.ShapeDtypeStruct((rows,) + places.shape[1:], places.dtype),
            jax.ShapeDtypeStruct((cols,) + places.shape[1:], places.dtype),
            jax.ShapeDtypeStruct((cols,) + omega.shape[1:], omega.dtype),
        ],
        in_specs=[pl.BlockSpec(memory_space=VMEM)] * 2,
        out_specs=[pl.BlockSpec(memory_space=VMEM)] * 3,
        scratch_shapes=[
            pltpu.SemaphoreType.DMA((3,)),
            pltpu.SemaphoreType.DMA((rows,)), pltpu.SemaphoreType.DMA((rows,)),
            pltpu.SemaphoreType.DMA((cols,)), pltpu.SemaphoreType.DMA((cols,)),
            pltpu.SemaphoreType.DMA((cols,)), pltpu.SemaphoreType.DMA((cols,)),
        ],
        compiler_params=pltpu.CompilerParams(collective_id=0, has_side_effects=True),
        name="gather_all",
    )(places, omega)


def split(x):
    hi = x.astype(jnp.bfloat16)
    rest = x - hi.astype(jnp.float32)
    mid = rest.astype(jnp.bfloat16)
    low = (rest - mid.astype(jnp.float32)).astype(jnp.bfloat16)
    return hi, mid, low


def target_features(spots, row8):
    n = spots.shape[1]
    coords = jnp.concatenate([spots[0:3], jnp.zeros((5, n), jnp.float32)], axis=0)
    centre = jnp.sum(coords, axis=1, keepdims=True) * (1.0 / n)
    moved = coords - centre
    norm = jnp.sum(moved * moved, axis=0, keepdims=True) + soft_sq
    feats = jnp.where(row8 == 3, norm, jnp.where(row8 == 4, 1.0, -2.0 * moved))
    hi, mid, low = (v.astype(jnp.float32) for v in split(feats))
    stack = jnp.concatenate([hi, mid, low, hi, mid, hi], axis=0)
    return stack.T.astype(jnp.bfloat16), centre


def source_features(base, scale, centre, row8):
    moved = base - centre
    norm = jnp.sum(moved * moved, axis=0, keepdims=True)
    feats = scale * jnp.where(row8 == 3, 1.0, jnp.where(row8 == 4, norm, moved))
    hi, mid, low = (v.astype(jnp.float32) for v in split(feats))
    return jnp.concatenate([hi, hi, hi, mid, mid, low], axis=0).astype(jnp.bfloat16)


def tile_kernel(codes_ref, tgt_ref, src_ref, omegas_ref, tiles_ref, sketch_ref,
                feat_ref, centre_ref, base_ref, scale_ref):
    step = pl.program_id(0)
    tgt_count, src_count = tgt_ref.shape[0], src_ref.shape[0]
    n = tgt_ref.shape[2]
    row8 = lax.broadcasted_iota(jnp.int32, (8, n), 0)

    @pl.when(step == 0)
    def _():
        sketch_ref[...] = jnp.zeros_like(sketch_ref)

        def prepare_target(t, carry):
            feats, centre = target_features(tgt_ref[t], row8)
            feat_ref[t] = feats
            centre_ref[t] = jnp.broadcast_to(centre, (8, n))
            return carry

        def prepare_source(s, carry):
            spots = src_ref[s]
            base_ref[s] = jnp.concatenate([spots[0:3], jnp.zeros((5, n), jnp.float32)], axis=0)
            weight = spots[3:4]
            scale_ref[s] = jnp.broadcast_to(1.0 / (weight * weight), (8, n))
            return carry

        lax.fori_loop(0, tgt_count, prepare_target, 0)
        lax.fori_loop(0, src_count, prepare_source, 0)

    @pl.when(codes_ref[step * GROUP] >= 0)
    def _():
        for g in range(GROUP):
            code = codes_ref[step * GROUP + g]
            live = (code >= 0).astype(jnp.float32)
            code = jnp.maximum(code, 0)
            t, s = code // src_count, code % src_count
            source = source_features(base_ref[s], scale_ref[s], centre_ref[t], row8)
            dist = jnp.dot(feat_ref[t], source, preferred_element_type=jnp.float32)
            tile = lax.rsqrt(dist).astype(jnp.bfloat16)
            tiles_ref[g] = tile
            part = lax.dot_general(omegas_ref[s], tile, (((1,), (1,)), ((), ())),
                                   preferred_element_type=jnp.float32)
            sketch_ref[t] += part * live


def tiles_and_sketch(codes, tgt, src, omegas):
    slots = codes.shape[0]
    tgt_count, src_count, n = tgt.shape[0], src.shape[0], tgt.shape[2]
    rank = omegas.shape[1]
    steps = slots // GROUP
    grid_spec = pltpu.PrefetchScalarGridSpec(
        num_scalar_prefetch=1,
        grid=(steps,),
        in_specs=[pl.BlockSpec(memory_space=VMEM)] * 3,
        out_specs=[
            pl.BlockSpec((GROUP, n, n), lambda i, codes: (jnp.where(codes[i * GROUP] >= 0, i, steps), 0, 0)),
            pl.BlockSpec(memory_space=VMEM),
        ],
        scratch_shapes=[
            VMEM((tgt_count, n, 48), jnp.bfloat16), VMEM((tgt_count, 8, n), jnp.float32),
            VMEM((src_count, 8, n), jnp.float32), VMEM((src_count, 8, n), jnp.float32),
        ],
    )
    return pl.pallas_call(
        tile_kernel,
        grid_spec=grid_spec,
        out_shape=[
            jax.ShapeDtypeStruct((slots + GROUP, n, n), jnp.bfloat16),
            jax.ShapeDtypeStruct((tgt_count, rank, n), jnp.float32),
        ],
        compiler_params=pltpu.CompilerParams(vmem_limit_bytes=40 << 20),
        name="tiles_and_sketch",
    )(codes, tgt, src, omegas)


def factor(sketch, left, out):
    rank = sketch.shape[0]
    gram = lax.dot_general(sketch, sketch, (((1,), (1,)), ((), ())),
                           precision=lax.Precision.HIGHEST, preferred_element_type=jnp.float32)
    energy = jnp.sum(jnp.sum(sketch * sketch, axis=0, keepdims=True), axis=1, keepdims=True)
    shift = ridge * energy / rank
    eye = (lax.broadcasted_iota(jnp.int32, (rank, rank), 0)
           == lax.broadcasted_iota(jnp.int32, (rank, rank), 1))
    mat = gram + jnp.where(eye, shift, 0.0)
    for b in range(0, rank, 8):
        rows = rank - b
        width = sketch.shape[1]
        row_at = lax.broadcasted_iota(jnp.int32, (rows, 1), 0)
        columns = [jnp.broadcast_to(mat[:, b + j:b + j + 1], (rows, 128)) for j in range(8)]
        for k in range(8):
            inv = lax.rsqrt(columns[k][k:k + 1, :])
            inv_wide = jnp.concatenate([inv] * (width // 128), axis=1)
            mult = jnp.where(row_at > k, columns[k] * inv, 0.0)
            mult_wide = jnp.concatenate([mult] * (width // 128), axis=1)
            mat_row = mat[k:k + 1, :] * inv[:, :rank]
            sketch_row = sketch[k:k + 1, :] * inv_wide
            out[b + k:b + k + 1, :] = sketch_row
            for j in range(k + 1, 8):
                columns[j] = columns[j] - mult * (columns[j][k:k + 1, :] * inv)
            mat = mat - mult[:, :rank] * mat_row
            sketch = sketch - mult_wide * sketch_row
        mat, sketch = mat[8:], sketch[8:]


def reduce_kernel(rows, sketch_ref, bases_ref, all_ref, pair_ref, sum_ref, far_ref, basis_ref,
                  pair_sem, far_send, far_recv, own_sem, out_send, out_recv):
    row, col = lax.axis_index("row"), lax.axis_index("col")
    core = lax.rem(row, 2)
    chip = row // 2
    chips = rows // 2
    partner = row + 1 - 2 * core
    barrier = pltpu.get_barrier_semaphore()
    for k in range(1, rows):
        pl.semaphore_signal(barrier, inc=1, device_id=(lax.rem(row + k, rows), col), device_id_type=MESH)
    pl.semaphore_wait(barrier, rows - 1)

    swap = pltpu.make_async_remote_copy(
        src_ref=sketch_ref.at[:, 1 - core], dst_ref=pair_ref, send_sem=pair_sem.at[0],
        recv_sem=pair_sem.at[1], device_id=(partner, col), device_id_type=MESH)
    swap.start()
    swap.wait()

    def far_copy(k, slot):
        peer = lax.rem(chip + k, chips)
        return pltpu.make_async_remote_copy(
            src_ref=sum_ref.at[peer], dst_ref=far_ref.at[slot], send_sem=far_send.at[k],
            recv_sem=far_recv.at[k], device_id=(peer * 2 + core, col), device_id_type=MESH)

    for k in range(1, chips):
        peer = lax.rem(chip + k, chips)
        sum_ref[peer] = sketch_ref[peer, core] + pair_ref[peer]
        far_copy(k, k).start()
    total = sketch_ref[chip, core] + pair_ref[chip]
    for k in range(1, chips):
        far_copy(k, k).wait_recv()
        total += far_ref[k]
    factor(total, None, basis_ref)
    basis = basis_ref[...]
    bases_ref[0] = basis * math.sqrt(basis.shape[1])
    all_ref[row] = basis.astype(jnp.bfloat16)

    def out_copy(k, slot):
        return pltpu.make_async_remote_copy(
            src_ref=all_ref.at[slot], dst_ref=all_ref.at[slot], send_sem=out_send.at[k],
            recv_sem=out_recv.at[k], device_id=(lax.rem(row + k, rows), col), device_id_type=MESH)

    for k in range(1, rows):
        out_copy(k, row).start()
    for k in range(1, chips):
        far_copy(k, k).wait_send()
    for k in range(1, rows):
        out_copy(k, row).wait_send()
        out_copy(k, lax.rem(row + rows - k, rows)).wait_recv()


def reduce_and_factor(sketch):
    rows, rank, n = sketch.shape
    return pl.pallas_call(
        functools.partial(reduce_kernel, rows),
        out_shape=[
            jax.ShapeDtypeStruct((1, rank, n), jnp.float32),
            jax.ShapeDtypeStruct((rows, rank, n), jnp.bfloat16),
        ],
        in_specs=[pl.BlockSpec(memory_space=VMEM)],
        out_specs=[pl.BlockSpec(memory_space=VMEM)] * 2,
        scratch_shapes=[
            VMEM((rows // 2, rank, n), jnp.float32),
            VMEM((rows // 2, rank, n), jnp.float32),
            VMEM((rows // 2, rank, n), jnp.float32),
            VMEM((rank, n), jnp.float32),
            pltpu.SemaphoreType.DMA((2,)),
            pltpu.SemaphoreType.DMA((rows // 2,)), pltpu.SemaphoreType.DMA((rows // 2,)),
            pltpu.SemaphoreType.DMA((1,)),
            pltpu.SemaphoreType.DMA((rows,)), pltpu.SemaphoreType.DMA((rows,)),
        ],
        compiler_params=pltpu.CompilerParams(collective_id=1, has_side_effects=True,
                                             vmem_limit_bytes=16 << 20),
        name="reduce_and_factor",
    )(sketch.reshape(rows // 2, 2, rank, n))


def project_kernel(codes_ref, tiles_ref, basis_ref, out_ref):
    step = pl.program_id(0)
    src_count = basis_ref.shape[0]
    first_live = codes_ref[step * GROUP] >= 0

    @pl.when(first_live)
    def _():
        for g in range(GROUP):
            code = codes_ref[step * GROUP + g]
            live = (code >= 0).astype(jnp.float32)
            t = jnp.maximum(code, 0) // src_count
            result = jnp.dot(basis_ref[t], tiles_ref[g], preferred_element_type=jnp.float32)
            out_ref[g] = (result * live).astype(jnp.bfloat16)

    @pl.when(jnp.logical_not(first_live))
    def _():
        out_ref[...] = jnp.zeros_like(out_ref)


def project(codes, tiles, basis_all):
    slots = codes.shape[0]
    rank, n = basis_all.shape[1], basis_all.shape[2]
    grid_spec = pltpu.PrefetchScalarGridSpec(
        num_scalar_prefetch=1,
        grid=(slots // GROUP,),
        in_specs=[
            pl.BlockSpec((GROUP, n, n), lambda i, codes: (jnp.where(codes[i * GROUP] >= 0, i, 0), 0, 0)),
            pl.BlockSpec(memory_space=VMEM),
        ],
        out_specs=pl.BlockSpec((GROUP, rank, n), lambda i, codes: (i, 0, 0)),
    )
    return pl.pallas_call(
        project_kernel,
        grid_spec=grid_spec,
        out_shape=jax.ShapeDtypeStruct((slots, rank, n), jnp.bfloat16),
        compiler_params=pltpu.CompilerParams(vmem_limit_bytes=24 << 20),
        name="project",
    )(codes, tiles, basis_all)


def body(places, omega, pairs):
    rows, cols = lax.axis_size("row"), lax.axis_size("col")
    codes = jnp.where(pairs[:, 0] >= 0, pairs[:, 0] // cols * cols + pairs[:, 1] % cols, -1)
    tgt, src, omegas = gather_all(places, omega, rows, cols)
    tiles, sketch = tiles_and_sketch(codes, tgt, src, omegas)
    bases, basis_all = reduce_and_factor(sketch)
    coeffs = project(codes, tiles, basis_all)
    return (bases, coeffs)


def solution(mesh):
    in_specs = (
        P(("row", "col"), None, None),
        P(("row", "col"), None, None),
        P(("row", "col"), None),
    )
    out_specs = (P(("row", "col"), None, None), P(("row", "col"), None, None))
    return jax.shard_map(body, mesh=mesh, in_specs=in_specs, out_specs=out_specs, check_vma=False)
```

time: 297 us -> 101 us (0.34); the launches traced: 292 us -> 100 us
  blocking collectives: 112 us -> 0 us
  Pallas kernels: 0 us -> 89.7 us
  waiting for transfers between devices: 66.1 us -> 0 us
  matrix products: 59.3 us -> 0 us
  other arithmetic: 19.4 us -> 0.77 us
  between operations: 15.4 us -> 0.67 us
  local copies, waits for them, and re-layouts: 17.5 us -> 9.25 us
    all_gather x4 -> x0, blocking collectives: 112 us -> none  [the longest x1 37 us: body(): src_places = lax.all_gather(places, 'col', axis=0, tiled=True)]
    pallas_call x0 -> x4, Pallas kernels: none -> 89.7 us  [the longest x1 33.5 us: reduce_and_factor(): pl.pallas_call(functools.partial(reduce_kernel, rows), out_shape=[jax.Sha...]
    reduce_scatter x1 -> x0, waiting for transfers between devices: 66.1 us -> none  [body(): lax.psum_scatter(partial_sketch, 'row', scatter_dimension=0, tiled=True)]
    dot_general x24 -> x0, matrix products: 57.5 us -> none  [the longest x16 33.1 us: one_source(): jnp.einsum('rj,tij->tri', panel, kernel, preferred_element_type=jnp.float32)]
    gather x21 -> x0, local copies, waits for them, and re-layouts: 12.4 us -> none  [the longest x7 4.15 us: projection_update(): jnp.take(tgt_places, tgt_group, axis=0)]
    another operation x5 -> x0, other arithmetic: 12.1 us -> none  [the longest x3 6.52 us: factor(): lower = jnp.linalg.cholesky(gram)]
    unnamed x3 -> x9, local copies, waits for them, and re-layouts: 0.98 us -> 9.25 us
    reduce_sum x18 -> x0, other arithmetic: 4.76 us -> none  [the longest x16 1.88 us: one_source(): weight = jnp.sum(hits.astype(jnp.float32), axis=1)]
  transfers between devices with their start and end apart: 1 -> 0, of which waited for: 1 -> 0; matrix products, arithmetic and copies ran while one was open for 0% -> 0% of each run, Pallas kernels for 0% -> 0%
where the time goes in v1:
time: 101 us; the launch traced here: 100 us
  Pallas kernels  89.7 us (89%)
  local copies, waits for them, and re-layouts  9.25 us (9%)
    pallas_call x1, Pallas kernels, reduce_and_factor(): pl.pallas_call(functools.partial(reduce_kernel, rows), out_shape=[jax.Sha...  33.5 us
    pallas_call x1, Pallas kernels, gather_all(): pl.pallas_call(functools.partial(gather_kernel, rows, cols), out_shape=[j...  26.6 us
    pallas_call x1, Pallas kernels, tiles_and_sketch(): pl.pallas_call(tile_kernel, grid_spec=grid_spec, out_shape=[jax.ShapeDtyp...  16.5 us
    pallas_call x1, Pallas kernels, project(): pl.pallas_call(project_kernel, grid_spec=grid_spec, out_shape=jax.ShapeDt...  13 us
    unnamed x9, local copies, waits for them, and re-layouts  9.25 us

profile of v1, /device:TPU:1, one launch (start us, length us, event | category | flops | bytes accessed | tf_op | source)
XLA Modules:
  0.0 100.4 jit_solution(2149078762092327833)
XLA Ops:
  0.6 0.8 compare_select_fusion.2.codes_ref
  1.4 26.6 %gather_all.1 = (f32[16,4,256]{2,1,0:T(4,128)}, f32[16,4,256]{2,1,0:T(4,128)}, bf16[16,64,256]{2,1,0:T(8,128)(2,1)}) custom-call(f32[1,4,256]{2,1,0:T(4,128)} %places_ref.1, bf16[1,64,256]{2,1,0:T(8,128)(2,1)} %omega_ref.1), custom_call_target="tpu_custom_call" | custom-call | tf_op jit(solution)/shard_map/gather_all/pallas_call | solution.py:66
  28.0 0.0 copy-start.1
  28.0 1.0 %copy-done.1 = bf16[16,64,256]{2,1,0:T(8,128)(2,1)S(1)} copy-done((bf16[16,64,256]{2,1,0:T(8,128)(2,1)S(1)}, bf16[16,64,256]{2,1,0:T(8,128)(2,1)}, u32[]{:S(2)}) %copy-start.1) | copy-done | bytes 524312
  29.1 0.0 copy-start.2
  29.1 0.8 copy-done.2
  29.9 0.0 copy-start.3
  29.9 0.8 copy-done.3
  30.7 16.5 %tiles_and_sketch.1 = (bf16[132,256,256]{2,1,0:T(8,128)(2,1)}, f32[16,64,256]{2,1,0:T(8,128)S(1)}) custom-call(s32[128]{0:T(128)S(1)} %compare_select_fusion.2.codes_ref, f32[16,4,256]{2,1,0:T(4,128)S(1)} %copy-done.2, f32[16,4,256]{2,1,0:T(4,128)S(1)} %copy-done.3, bf16[16,64,256]{2,1,0:T(8,128)(2,1)S(1)} %copy-done.1), custom_call_target="tpu_custom_call" | custom-call | tf_op jit(solution)/shard_map/tiles_and_sketch/pallas_call | solution.py:175
  47.2 33.5 %reduce_and_factor.1 = (f32[1,64,256]{2,1,0:T(8,128)S(1)}, bf16[16,64,256]{2,1,0:T(8,128)(2,1)S(1)}) custom-call(f32[8,2,64,256]{3,2,1,0:T(8,128)S(1)} %bitcast.14), custom_call_target="tpu_custom_call" | custom-call | tf_op jit(solution)/shard_map/reduce_and_factor/pallas_call | solution.py:269
  80.8 0.0 copy-start
  80.8 5.9 %copy-done = bf16[132,256,256]{2,1,0:T(8,128)(2,1)S(1)} copy-done((bf16[132,256,256]{2,1,0:T(8,128)(2,1)S(1)}, bf16[132,256,256]{2,1,0:T(8,128)(2,1)}, u32[]{:S(2)}) %copy-start) | copy-done | bytes 17301528
  86.7 13.0 %project.1 = bf16[128,64,256]{2,1,0:T(8,128)(2,1)} custom-call(s32[128]{0:T(128)S(1)} %compare_select_fusion.2.codes_ref, bf16[132,256,256]{2,1,0:T(8,128)(2,1)S(1)} %copy-done, bf16[16,64,256]{2,1,0:T(8,128)(2,1)S(1)} %get-tuple-element.15.basis_ref), custom_call_target="tpu_custom_call" | custom-call | tf_op jit(solution)/shard_map/project/pallas_call | solution.py:324
  99.7 0.6 copy.6
Async XLA Ops:
  28.0 1.0 %copy-start.1 = (bf16[16,64,256]{2,1,0:T(8,128)(2,1)S(1)}, bf16[16,64,256]{2,1,0:T(8,128)(2,1)}, u32[]{:S(2)}) copy-start(bf16[16,64,256]{2,1,0:T(8,128)(2,1)} %get-tuple-element.11.omegas_ref) | copy-start | bytes 1572868
  29.1 0.8 copy-start.2
  29.9 0.8 copy-start.3
  80.8 5.9 %copy-start = (bf16[132,256,256]{2,1,0:T(8,128)(2,1)S(1)}, bf16[132,256,256]{2,1,0:T(8,128)(2,1)}, u32[]{:S(2)}) copy-start(bf16[132,256,256]{2,1,0:T(8,128)(2,1)} %get-tuple-element.14.tiles_ref) | copy-start | bytes 51904516

commit v2 on v0

v2 whole, which is shorter than its diff:
```python
import functools
import math

import jax
import jax.numpy as jnp
from jax import lax
from jax.experimental import pallas as pl
from jax.experimental.pallas import tpu as pltpu
from jax.sharding import PartitionSpec as P

soft_sq = 0.09
ridge = 0.05
MESH = pl.DeviceIdType.MESH
VMEM = pltpu.VMEM
SMEM = pltpu.SMEM
DMA = pltpu.SemaphoreType.DMA
GROUP = 8
NT = (((1,), (1,)), ((), ()))


def slots_kernel(cols, pairs_ref, meta_ref):
    slots = pairs_ref.shape[1]
    tgt_row = jnp.broadcast_to(pairs_ref[0:1], (slots, slots))
    src_row = jnp.broadcast_to(pairs_ref[1:2], (8, slots))
    tgt = tgt_row.T
    at_col = lax.broadcasted_iota(jnp.int32, (slots, slots), 0)
    at_row = lax.broadcasted_iota(jnp.int32, (slots, slots), 1)
    same = (tgt == tgt_row) & (tgt >= 0) & (at_col < at_row)
    last_of = (tgt >= 0) & (tgt // cols == at_row)

    def top(mask):
        best = jnp.where(mask, at_col, -1)
        rows = slots
        while rows > 8:
            rows //= 2
            best = jnp.maximum(best[:rows], best[rows:])
        for shift in (4, 2, 1):
            best = jnp.maximum(best, pltpu.roll(best, shift, 0))
        return jnp.where(best < 0, slots, best)

    live = tgt_row[0:8] >= 0
    code = jnp.where(live, tgt_row[0:8] // cols * cols + src_row % cols, 0)
    row = lax.broadcasted_iota(jnp.int32, (8, slots), 0)
    meta = jnp.where(row == 0, code, jnp.where(row == 1, top(same), top(last_of)))
    meta_ref[...] = jnp.where(row == 3, live.astype(jnp.int32), meta)


def slot_table(pairs, cols):
    return pl.pallas_call(
        functools.partial(slots_kernel, cols),
        out_shape=jax.ShapeDtypeStruct((8, pairs.shape[1]), jnp.int32),
        in_specs=[pl.BlockSpec(memory_space=VMEM)],
        out_specs=pl.BlockSpec(memory_space=VMEM),
        name="slot_table",
    )(pairs)


def split(x):
    hi = x.astype(jnp.bfloat16).astype(jnp.float32)
    rest = x - hi
    mid = rest.astype(jnp.bfloat16).astype(jnp.float32)
    return hi, mid, rest - mid


def target_features(spots, row8):
    n = spots.shape[1]
    coords = jnp.concatenate([spots[0:3], jnp.zeros((5, n), jnp.float32)], axis=0)
    centre = jnp.sum(coords, axis=1, keepdims=True) * (1.0 / n)
    moved = coords - centre
    norm = jnp.sum(moved * moved, axis=0, keepdims=True) + soft_sq
    feats = jnp.where(row8 == 3, norm, jnp.where(row8 == 4, 1.0, -2.0 * moved))
    hi, mid, low = split(feats)
    stack = jnp.concatenate([hi, mid, low, hi, mid, hi], axis=0)
    return stack.T.astype(jnp.bfloat16), centre


def source_features(base, scale, centre, row8):
    moved = base - centre
    norm = jnp.sum(moved * moved, axis=0, keepdims=True)
    feats = scale * jnp.where(row8 == 3, 1.0, jnp.where(row8 == 4, norm, moved))
    hi, mid, low = split(feats)
    return jnp.concatenate([hi, hi, hi, mid, mid, low], axis=0).astype(jnp.bfloat16)


def prepare(tgt_ref, src_ref, feat_ref, centre_ref, base_ref, scale_ref):
    n = tgt_ref.shape[2]
    row8 = lax.broadcasted_iota(jnp.int32, (8, n), 0)

    def prepare_target(t, carry):
        feats, centre = target_features(tgt_ref[t], row8)
        feat_ref[t] = feats
        centre_ref[t] = jnp.broadcast_to(centre, (8, n))
        return carry

    def prepare_source(s, carry):
        spots = src_ref[s]
        base_ref[s] = jnp.concatenate([spots[0:3], jnp.zeros((5, n), jnp.float32)], axis=0)
        weight = spots[3:4]
        scale_ref[s] = jnp.broadcast_to(1.0 / (weight * weight), (8, n))
        return carry

    lax.fori_loop(0, tgt_ref.shape[0], prepare_target, 0, unroll=4)
    lax.fori_loop(0, src_ref.shape[0], prepare_source, 0, unroll=4)


def tile_group(first, cols, meta_ref, feat_ref, centre_ref, base_ref, scale_ref, tiles_ref):
    n = feat_ref.shape[1]
    row8 = lax.broadcasted_iota(jnp.int32, (8, n), 0)
    for g in range(GROUP):
        code = meta_ref[0, first + g]
        t, s = code // cols, code % cols
        source = source_features(base_ref[s], scale_ref[s], centre_ref[t], row8)
        dist = jnp.dot(feat_ref[t], source, preferred_element_type=jnp.float32)
        tiles_ref[first + g] = lax.rsqrt(dist).astype(jnp.bfloat16)


def sketch_group(first, cols, meta_ref, omegas_ref, tiles_ref, running_ref):
    parts = []
    for g in range(GROUP):
        s = meta_ref[0, first + g] % cols
        live = meta_ref[3, first + g].astype(jnp.float32)
        part = lax.dot_general(omegas_ref[s], tiles_ref[first + g], NT, preferred_element_type=jnp.float32)
        parts.append(part * live)
    for g in range(GROUP):
        running_ref[first + g] = running_ref[meta_ref[1, first + g]] + parts[g]


def factor(sketch, out):
    rank, width = sketch.shape
    gram = lax.dot_general(sketch, sketch, NT, precision=lax.Precision.HIGHEST,
                           preferred_element_type=jnp.float32)
    energy = jnp.sum(jnp.sum(sketch * sketch, axis=0, keepdims=True), axis=1, keepdims=True)
    shift = ridge * energy / rank
    eye = (lax.broadcasted_iota(jnp.int32, (rank, rank), 0)
           == lax.broadcasted_iota(jnp.int32, (rank, rank), 1))
    mat = gram + jnp.where(eye, shift, 0.0)
    for b in range(0, rank, 8):
        rows = rank - b
        row_at = lax.broadcasted_iota(jnp.int32, (rows, 1), 0)
        columns = [jnp.broadcast_to(mat[:, b + j:b + j + 1], (rows, 128)) for j in range(8)]
        for k in range(8):
            inv = lax.rsqrt(columns[k][k:k + 1, :])
            inv_wide = jnp.concatenate([inv] * (width // 128), axis=1)
            mult = jnp.where(row_at > k, columns[k] * inv, 0.0)
            mult_wide = jnp.concatenate([mult] * (width // 128), axis=1)
            mat_row = mat[k:k + 1, :] * inv[:, :rank]
            sketch_row = sketch[k:k + 1, :] * inv_wide
            out[b + k:b + k + 1, :] = sketch_row
            for j in range(k + 1, 8):
                columns[j] = columns[j] - mult * (columns[j][k:k + 1, :] * inv)
            mat = mat - mult[:, :rank] * mat_row
            sketch = sketch - mult_wide * sketch_row
        mat, sketch = mat[8:], sketch[8:]


def sketch_kernel(rows, cols, meta_ref, places_ref, omega_ref, tiles_out, bases_ref, all_ref,
                  tgt_ref, src_ref, omegas_ref, feat_ref, centre_ref, base_ref, scale_ref,
                  tiles_ref, running_ref, stage_ref, pair_ref, sum_ref, far_ref, basis_ref,
                  own_sem, row_send, row_recv, col_send, col_recv, om_send, om_recv, tile_sem,
                  pair_send, pair_recv, far_send, far_recv, out_send, out_recv, relay_send, relay_recv):
    row, col = lax.axis_index("row"), lax.axis_index("col")
    core, chip, chips = lax.rem(row, 2), row // 2, rows // 2
    partner = row + 1 - 2 * core
    slots = tiles_ref.shape[0]
    groups = slots // GROUP

    barrier = pltpu.get_barrier_semaphore()
    for k in range(1, cols):
        pl.semaphore_signal(barrier, inc=1, device_id=(row, lax.rem(col + k, cols)), device_id_type=MESH)
    for k in range(1, rows):
        pl.semaphore_signal(barrier, inc=1, device_id=(lax.rem(row + k, rows), col), device_id_type=MESH)
    own = [
        pltpu.make_async_copy(places_ref, tgt_ref.at[pl.ds(row, 1)], own_sem.at[0]),
        pltpu.make_async_copy(places_ref, src_ref.at[pl.ds(col, 1)], own_sem.at[1]),
        pltpu.make_async_copy(omega_ref, omegas_ref.at[pl.ds(col, 1)], own_sem.at[2]),
    ]
    for c in own:
        c.start()
    running_ref[slots] = jnp.zeros_like(running_ref[slots])
    for c in own:
        c.wait()
    pl.semaphore_wait(barrier, rows + cols - 2)

    def row_copy(k, slot):
        return pltpu.make_async_remote_copy(
            src_ref=tgt_ref.at[pl.ds(row, 1)], dst_ref=tgt_ref.at[pl.ds(slot, 1)], send_sem=row_send.at[k],
            recv_sem=row_recv.at[k], device_id=(lax.rem(row + k, rows), col), device_id_type=MESH)

    def col_copy(k, slot):
        return pltpu.make_async_remote_copy(
            src_ref=src_ref.at[pl.ds(col, 1)], dst_ref=src_ref.at[pl.ds(slot, 1)], send_sem=col_send.at[k],
            recv_sem=col_recv.at[k], device_id=(row, lax.rem(col + k, cols)), device_id_type=MESH)

    def om_copy(k, slot):
        return pltpu.make_async_remote_copy(
            src_ref=omegas_ref.at[pl.ds(col, 1)], dst_ref=omegas_ref.at[pl.ds(slot, 1)], send_sem=om_send.at[k],
            recv_sem=om_recv.at[k], device_id=(row, lax.rem(col + k, cols)), device_id_type=MESH)

    for k in range(1, cols):
        col_copy(k, col).start()
    for k in range(1, rows):
        row_copy(k, row).start()
    for k in range(1, cols):
        om_copy(k, col).start()
    for k in range(1, rows):
        row_copy(k, lax.rem(row + rows - k, rows)).wait()
    for k in range(1, cols):
        col_copy(k, lax.rem(col + cols - k, cols)).wait()
    prepare(tgt_ref, src_ref, feat_ref, centre_ref, base_ref, scale_ref)

    def tile_copy(i):
        part = pl.ds(i * GROUP, GROUP)
        return pltpu.make_async_copy(tiles_ref.at[part], tiles_out.at[part], tile_sem.at[i])

    def tile_step(i, carry):
        tile_group(i * GROUP, cols, meta_ref, feat_ref, centre_ref, base_ref, scale_ref, tiles_ref)
        tile_copy(i).start()
        return carry

    lax.fori_loop(0, groups, tile_step, 0)
    for k in range(1, cols):
        om_copy(k, lax.rem(col + cols - k, cols)).wait()

    def sketch_step(i, carry):
        sketch_group(i * GROUP, cols, meta_ref, omegas_ref, tiles_ref, running_ref)
        return carry

    lax.fori_loop(0, groups, sketch_step, 0)

    def pair_copy(c):
        return pltpu.make_async_remote_copy(
            src_ref=stage_ref.at[c], dst_ref=pair_ref.at[c], send_sem=pair_send.at[c],
            recv_sem=pair_recv.at[c], device_id=(partner, col), device_id_type=MESH)

    half = chips // 2

    def far_chip(k):
        return lax.rem(chip // half + k // half, 2) * half + lax.rem(lax.rem(chip, half) + k % half, half)

    def back_chip(k):
        return lax.rem(chip // half + k // half, 2) * half + lax.rem(lax.rem(chip, half) + half - k % half, half)

    def far_copy(k):
        return pltpu.make_async_remote_copy(
            src_ref=sum_ref.at[k], dst_ref=far_ref.at[k], send_sem=far_send.at[k],
            recv_sem=far_recv.at[k], device_id=(far_chip(k) * 2 + core, col), device_id_type=MESH)

    order = sorted(range(1, chips), key=lambda k: -(k // half + min(k % half, half - k % half)))
    for k in order + [0]:
        c = far_chip(k)
        stage_ref[c] = running_ref[meta_ref[2, 2 * c + 1 - core]]
        pair_copy(c).start()
    for k in order + [0]:
        c = far_chip(k)
        sum_ref[k] = running_ref[meta_ref[2, 2 * c + core]]
    for k in order + [0]:
        c = far_chip(k)
        pair_copy(c).wait_recv()
        sum_ref[k] += pair_ref[c]
        if k:
            far_copy(k).start()
    total = sum_ref[0]
    for k in reversed(order):
        far_copy(k).wait_recv()
        total += far_ref[k]
    factor(total, basis_ref)
    basis = basis_ref[...]
    all_ref[row] = basis.astype(jnp.bfloat16)

    def out_copy(k, slot):
        return pltpu.make_async_remote_copy(
            src_ref=all_ref.at[slot], dst_ref=all_ref.at[slot], send_sem=out_send.at[k],
            recv_sem=out_recv.at[k], device_id=(far_chip(k) * 2 + core, col), device_id_type=MESH)

    def relay_copy(k, slot):
        return pltpu.make_async_remote_copy(
            src_ref=all_ref.at[slot], dst_ref=all_ref.at[slot], send_sem=relay_send.at[k],
            recv_sem=relay_recv.at[k], device_id=(partner, col), device_id_type=MESH)

    for k in order:
        out_copy(k, row).start()
    relay_copy(0, row).start()
    bases_ref[0] = basis * math.sqrt(basis.shape[1])
    for c in range(chips):
        pair_copy(c).wait_send()
    for k in order:
        far_copy(k).wait_send()
    for i in range(groups):
        tile_copy(i).wait()
    for k in reversed(order):
        slot = back_chip(k) * 2 + core
        out_copy(k, slot).wait_recv()
        relay_copy(k, slot).start()
    for k in order:
        out_copy(k, row).wait_send()
    for k in [0] + order[::-1]:
        slot = back_chip(k) * 2 + core
        relay_copy(k, slot).wait_send()
        relay_copy(k, slot + 1 - 2 * core).wait_recv()


def sketch_and_factor(meta, places, omega, rows, cols):
    slots = meta.shape[1]
    rank, n = omega.shape[1], omega.shape[2]
    chips = rows // 2
    bf16, f32 = jnp.bfloat16, jnp.float32
    return pl.pallas_call(
        functools.partial(sketch_kernel, rows, cols),
        out_shape=[
            jax.ShapeDtypeStruct((slots, n, n), bf16),
            jax.ShapeDtypeStruct((1, rank, n), f32),
            jax.ShapeDtypeStruct((rows, rank, n), bf16),
        ],
        in_specs=[pl.BlockSpec(memory_space=SMEM)] + [pl.BlockSpec(memory_space=pl.ANY)] * 2,
        out_specs=[pl.BlockSpec(memory_space=pl.ANY)] + [pl.BlockSpec(memory_space=VMEM)] * 2,
        scratch_shapes=[
            VMEM((rows,) + places.shape[1:], f32), VMEM((cols,) + places.shape[1:], f32),
            VMEM((cols, rank, n), bf16),
            VMEM((rows, n, 48), bf16), VMEM((rows, 8, n), f32),
            VMEM((cols, 8, n), f32), VMEM((cols, 8, n), f32),
            VMEM((slots, n, n), bf16), VMEM((slots + 1, rank, n), f32),
            VMEM((chips, rank, n), f32), VMEM((chips, rank, n), f32),
            VMEM((chips, rank, n), f32), VMEM((chips, rank, n), f32),
            VMEM((rank, n), f32),
            DMA((3,)), DMA((rows,)), DMA((rows,)), DMA((cols,)), DMA((cols,)), DMA((cols,)), DMA((cols,)),
            DMA((slots // GROUP,)),
            DMA((chips,)), DMA((chips,)), DMA((chips,)), DMA((chips,)),
            DMA((chips,)), DMA((chips,)), DMA((chips,)), DMA((chips,)),
        ],
        compiler_params=pltpu.CompilerParams(collective_id=0, has_side_effects=True,
                                             vmem_limit_bytes=60 << 20),
        name="sketch_and_factor",
    )(meta, places, omega)


def project_kernel(cols, meta_ref, basis_ref, tiles_hbm, out_hbm, tiles_ref, out_ref, in_sem, out_sem):
    slots = tiles_ref.shape[0]
    groups = slots // GROUP

    def tile_copy(i):
        part = pl.ds(i * GROUP, GROUP)
        return pltpu.make_async_copy(tiles_hbm.at[part], tiles_ref.at[part], in_sem.at[i])

    def out_copy(i):
        part = pl.ds(i * GROUP, GROUP)
        return pltpu.make_async_copy(out_ref.at[part], out_hbm.at[part], out_sem.at[i])

    def start(i, carry):
        tile_copy(i).start()
        return carry

    def step(i, carry):
        tile_copy(i).wait()
        for g in range(GROUP):
            p = i * GROUP + g
            live = meta_ref[3, p].astype(jnp.float32)
            result = jnp.dot(basis_ref[meta_ref[0, p] // cols], tiles_ref[p],
                             preferred_element_type=jnp.float32)
            out_ref[p] = (result * live).astype(jnp.bfloat16)
        out_copy(i).start()
        return carry

    def finish(i, carry):
        out_copy(i).wait()
        return carry

    lax.fori_loop(0, groups, start, 0)
    lax.fori_loop(0, groups, step, 0)
    lax.fori_loop(0, groups, finish, 0)


def project(meta, tiles, basis_all, cols):
    slots = meta.shape[1]
    rank, n = basis_all.shape[1], basis_all.shape[2]
    return pl.pallas_call(
        functools.partial(project_kernel, cols),
        out_shape=jax.ShapeDtypeStruct((slots, rank, n), jnp.bfloat16),
        in_specs=[pl.BlockSpec(memory_space=SMEM), pl.BlockSpec(memory_space=VMEM),
                  pl.BlockSpec(memory_space=pl.ANY)],
        out_specs=pl.BlockSpec(memory_space=pl.ANY),
        scratch_shapes=[
            VMEM((slots, n, n), jnp.bfloat16), VMEM((slots, rank, n), jnp.bfloat16),
            DMA((slots // GROUP,)), DMA((slots // GROUP,)),
        ],
        compiler_params=pltpu.CompilerParams(vmem_limit_bytes=60 << 20),
        name="project",
    )(meta, basis_all, tiles)


def body(places, omega, pairs):
    rows, cols = lax.axis_size("row"), lax.axis_size("col")
    meta = slot_table(pairs.T, cols)
    tiles, bases, basis_all = sketch_and_factor(meta, places, omega, rows, cols)
    coeffs = project(meta, tiles, basis_all, cols)
    return (bases, coeffs)


def solution(mesh):
    in_specs = (
        P(("row", "col"), None, None),
        P(("row", "col"), None, None),
        P(("row", "col"), None),
    )
    out_specs = (P(("row", "col"), None, None), P(("row", "col"), None, None))
    return jax.shard_map(body, mesh=mesh, in_specs=in_specs, out_specs=out_specs, check_vma=False)
```

time: 297 us -> 65.3 us (0.22); the launches traced: 292 us -> 65 us
  blocking collectives: 112 us -> 0 us
  waiting for transfers between devices: 66.1 us -> 0 us
  Pallas kernels: 0 us -> 63.7 us
  matrix products: 59.3 us -> 0 us
  other arithmetic: 19.4 us -> 0 us
  local copies, waits for them, and re-layouts: 17.5 us -> 0.64 us
  between operations: 15.4 us -> 0.66 us
    all_gather x4 -> x0, blocking collectives: 112 us -> none  [the longest x1 37 us: body(): src_places = lax.all_gather(places, 'col', axis=0, tiled=True)]
    reduce_scatter x1 -> x0, waiting for transfers between devices: 66.1 us -> none  [body(): lax.psum_scatter(partial_sketch, 'row', scatter_dimension=0, tiled=True)]
    pallas_call x0 -> x3, Pallas kernels: none -> 63.7 us  [the longest x1 53 us: sketch_and_factor(): pl.pallas_call(functools.partial(sketch_kernel, rows, cols), out_shape=[j...]
    dot_general x24 -> x0, matrix products: 57.5 us -> none  [the longest x16 33.1 us: one_source(): jnp.einsum('rj,tij->tri', panel, kernel, preferred_element_type=jnp.float32)]
    gather x21 -> x0, local copies, waits for them, and re-layouts: 12.4 us -> none  [the longest x7 4.15 us: projection_update(): jnp.take(tgt_places, tgt_group, axis=0)]
    another operation x5 -> x0, other arithmetic: 12.1 us -> none  [the longest x3 6.52 us: factor(): lower = jnp.linalg.cholesky(gram)]
    reduce_sum x18 -> x0, other arithmetic: 4.76 us -> none  [the longest x16 1.88 us: one_source(): weight = jnp.sum(hits.astype(jnp.float32), axis=1)]
  transfers between devices with their start and end apart: 1 -> 0, of which waited for: 1 -> 0; matrix products, arithmetic and copies ran while one was open for 0% -> 0% of each run, Pallas kernels for 0% -> 0%
where the time goes in v2:
time: 65.3 us; the launch traced here: 65 us
  Pallas kernels  63.7 us (98%)
  between operations  0.66 us (1%)
    pallas_call x1, Pallas kernels, sketch_and_factor(): pl.pallas_call(functools.partial(sketch_kernel, rows, cols), out_shape=[j...  53 us
    pallas_call x1, Pallas kernels, project(): pl.pallas_call(functools.partial(project_kernel, cols), out_shape=jax.Sha...  9.32 us
    pallas_call x1, Pallas kernels, slot_table(): pl.pallas_call(functools.partial(slots_kernel, cols), out_shape=jax.Shape...  1.42 us

profile of v2, /device:TPU:1, one launch (start us, length us, event | category | flops | bytes accessed | tf_op | source)
XLA Modules:
  0.0 65.0 jit_solution(7538256599778935275)
XLA Ops:
  0.6 1.4 %slot_table.1.meta_ref = s32[8,128]{1,0:T(8,128)} custom-call(s32[2,128]{1,0:T(2,128)} %bitcast.1), custom_call_target="tpu_custom_call" | custom-call | tf_op jit(solution)/shard_map/slot_table/pallas_call | solution.py:49
  2.0 53.0 %sketch_and_factor.1 = (bf16[128,256,256]{2,1,0:T(8,128)(2,1)}, f32[1,64,256]{2,1,0:T(8,128)}, bf16[16,64,256]{2,1,0:T(8,128)(2,1)}) custom-call(s32[8,128]{1,0:T(8,128)} %slot_table.1.meta_ref, f32[1,4,256]{2,1,0:T(4,128)} %places_ref.1, bf16[1,64,256]{2,1,0:T(8,128)(2,1)} %omega_ref.1), custom_call_target="tpu_custom_call" | custom-call | tf_op jit(solution)/shard_map/sketch_and_factor/pallas_call | solution.py:307
  55.1 0.0 copy-start
  55.1 9.3 %project.1 = bf16[128,64,256]{2,1,0:T(8,128)(2,1)} custom-call(s32[8,128]{1,0:T(8,128)} %slot_table.1.meta_ref, bf16[16,64,256]{2,1,0:T(8,128)(2,1)} %get-tuple-element.6.basis_ref, bf16[128,256,256]{2,1,0:T(8,128)(2,1)} %get-tuple-element.7.tiles_hbm), custom_call_target="tpu_custom_call" | custom-call | tf_op jit(solution)/shard_map/project/pallas_call | solution.py:375
  64.4 0.0 copy-done
  64.4 0.6 copy.6
Async XLA Ops:
  55.1 9.3 %copy-start = (f32[1,64,256]{2,1,0:T(8,128)S(1)}, f32[1,64,256]{2,1,0:T(8,128)}, u32[]{:S(2)}) copy-start(f32[1,64,256]{2,1,0:T(8,128)} %get-tuple-element.10) | copy-start | bytes 196612

commit v3 on v2

v3 whole, which is shorter than its diff:
```python
import functools
import math

import jax
import jax.numpy as jnp
from jax import lax
from jax.experimental import pallas as pl
from jax.experimental.pallas import tpu as pltpu
from jax.sharding import PartitionSpec as P

soft_sq = 0.09
ridge = 0.05
MESH = pl.DeviceIdType.MESH
VMEM = pltpu.VMEM
SMEM = pltpu.SMEM
DMA = pltpu.SemaphoreType.DMA
GROUP = 16
NT = (((1,), (1,)), ((), ()))


def slot_table(cols, pairs_ref, meta_ref):
    slots = pairs_ref.shape[1]
    tgt_row = jnp.broadcast_to(pairs_ref[0:1], (slots, slots))
    src_row = jnp.broadcast_to(pairs_ref[1:2], (8, slots))
    tgt = tgt_row.T
    at_col = lax.broadcasted_iota(jnp.int32, (slots, slots), 0)
    at_row = lax.broadcasted_iota(jnp.int32, (slots, slots), 1)
    same = (tgt == tgt_row) & (tgt >= 0) & (at_col < at_row)
    last_of = (tgt >= 0) & (tgt // cols == at_row)

    def top(mask):
        best = jnp.where(mask, at_col, -1)
        rows = slots
        while rows > 8:
            rows //= 2
            best = jnp.maximum(best[:rows], best[rows:])
        for shift in (4, 2, 1):
            best = jnp.maximum(best, pltpu.roll(best, shift, 0))
        return jnp.where(best < 0, slots, best)

    live = tgt_row[0:8] >= 0
    code = jnp.where(live, tgt_row[0:8] // cols * cols + src_row % cols, 0)
    row = lax.broadcasted_iota(jnp.int32, (8, slots), 0)
    meta = jnp.where(row == 0, code, jnp.where(row == 1, top(same), top(last_of)))
    meta_ref[...] = jnp.where(row == 3, live.astype(jnp.int32), meta)


def split(x):
    hi = x.astype(jnp.bfloat16).astype(jnp.float32)
    rest = x - hi
    mid = rest.astype(jnp.bfloat16).astype(jnp.float32)
    return hi, mid, rest - mid


def target_features(spots, row8):
    n = spots.shape[1]
    coords = jnp.concatenate([spots[0:3], jnp.zeros((5, n), jnp.float32)], axis=0)
    centre = jnp.sum(coords, axis=1, keepdims=True) * (1.0 / n)
    moved = coords - centre
    norm = jnp.sum(moved * moved, axis=0, keepdims=True) + soft_sq
    feats = jnp.where(row8 == 3, norm, jnp.where(row8 == 4, 1.0, -2.0 * moved))
    hi, mid, low = split(feats)
    stack = jnp.concatenate([hi, mid, low, hi, mid, hi], axis=0)
    return stack.T.astype(jnp.bfloat16), centre


def source_features(base, scale, centre, row8):
    moved = base - centre
    norm = jnp.sum(moved * moved, axis=0, keepdims=True)
    feats = scale * jnp.where(row8 == 3, 1.0, jnp.where(row8 == 4, norm, moved))
    hi, mid, low = split(feats)
    return jnp.concatenate([hi, hi, hi, mid, mid, low], axis=0).astype(jnp.bfloat16)


def prepare_targets(tgt_ref, feat_ref, centre_ref):
    n = tgt_ref.shape[2]
    row8 = lax.broadcasted_iota(jnp.int32, (8, n), 0)

    def one(t, carry):
        feats, centre = target_features(tgt_ref[t], row8)
        feat_ref[t] = feats
        centre_ref[t] = jnp.broadcast_to(centre, (8, n))
        return carry

    lax.fori_loop(0, tgt_ref.shape[0], one, 0, unroll=4)


def prepare_sources(src_ref, base_ref, scale_ref):
    n = src_ref.shape[2]

    def one(s, carry):
        spots = src_ref[s]
        base_ref[s] = jnp.concatenate([spots[0:3], jnp.zeros((5, n), jnp.float32)], axis=0)
        weight = spots[3:4]
        scale_ref[s] = jnp.broadcast_to(1.0 / (weight * weight), (8, n))
        return carry

    lax.fori_loop(0, src_ref.shape[0], one, 0, unroll=4)


def tile_group(first, cols, meta_ref, feat_ref, centre_ref, base_ref, scale_ref, tiles_ref):
    n = feat_ref.shape[1]
    row8 = lax.broadcasted_iota(jnp.int32, (8, n), 0)
    for g in range(GROUP):
        code = meta_ref[0, first + g]
        t, s = code // cols, code % cols
        source = source_features(base_ref[s], scale_ref[s], centre_ref[t], row8)
        dist = jnp.dot(feat_ref[t], source, preferred_element_type=jnp.float32)
        tiles_ref[first + g] = lax.rsqrt(dist).astype(jnp.bfloat16)


def sketch_group(first, h, cols, meta_ref, omegas_ref, tiles_ref, running_ref):
    half = running_ref.shape[3]
    parts = []
    for g in range(GROUP):
        s = meta_ref[0, first + g] % cols
        live = meta_ref[3, first + g].astype(jnp.float32)
        part = lax.dot_general(omegas_ref[s], tiles_ref[first + g, h * half:(h + 1) * half], NT,
                               preferred_element_type=jnp.float32)
        parts.append(part * live)
    for g in range(GROUP):
        running_ref[h, first + g] = running_ref[h, meta_ref[1, first + g]] + parts[g]


def factor(sketch, out, at_half):
    rank, width = sketch.shape
    gram = lax.dot_general(sketch, sketch, NT, precision=lax.Precision.HIGHEST,
                           preferred_element_type=jnp.float32)
    energy = jnp.sum(jnp.sum(sketch * sketch, axis=0, keepdims=True), axis=1, keepdims=True)
    shift = ridge * energy / rank
    eye = (lax.broadcasted_iota(jnp.int32, (rank, rank), 0)
           == lax.broadcasted_iota(jnp.int32, (rank, rank), 1))
    mat = gram + jnp.where(eye, shift, 0.0)
    for b in range(0, rank, 8):
        rows = rank - b
        row_at = lax.broadcasted_iota(jnp.int32, (rows, 1), 0)
        columns = [jnp.broadcast_to(mat[:, b + j:b + j + 1], (rows, 128)) for j in range(8)]
        for k in range(8):
            inv = lax.rsqrt(columns[k][k:k + 1, :])
            inv_wide = jnp.concatenate([inv] * (width // 128), axis=1)
            mult = jnp.where(row_at > k, columns[k] * inv, 0.0)
            mult_wide = jnp.concatenate([mult] * (width // 128), axis=1)
            mat_row = mat[k:k + 1, :] * inv[:, :rank]
            sketch_row = sketch[k:k + 1, :] * inv_wide
            out[b + k:b + k + 1, :] = sketch_row
            for j in range(k + 1, 8):
                columns[j] = columns[j] - mult * (columns[j][k:k + 1, :] * inv)
            mat = mat - mult[:, :rank] * mat_row
            sketch = sketch - mult_wide * sketch_row
        mat, sketch = mat[8:], sketch[8:]
        if 2 * (b + 8) == rank:
            at_half()


def sketch_kernel(rows, cols, pairs_hbm, places_ref, omega_ref, tiles_ref, basis_ref, all_ref, table_ref,
                  pairs_ref, meta_ref, tgt_ref, src_ref, omegas_ref, feat_ref, centre_ref, base_ref, scale_ref,
                  running_ref, stage_ref, pair_ref, sum_ref, far_ref,
                  own_sem, row_send, row_recv, col_send, col_recv, om_send, om_recv,
                  pair_send, pair_recv, far_send, far_recv, out_send, out_recv, relay_send, relay_recv):
    row, col = lax.axis_index("row"), lax.axis_index("col")
    core, chip, chips = lax.rem(row, 2), row // 2, rows // 2
    partner = row + 1 - 2 * core
    slots = tiles_ref.shape[0]
    groups = slots // GROUP
    rank, half = running_ref.shape[2], running_ref.shape[3]
    ring, depth = chips // 2, cols // 2

    def moved(at, k, size):
        return lax.rem(at // size + k // size, 2) * size + lax.rem(lax.rem(at, size) + k % size, size)

    def moved_back(at, k, size):
        return lax.rem(at // size + k // size, 2) * size + lax.rem(lax.rem(at, size) + size - k % size, size)

    far = sorted(range(1, chips), key=lambda k: -(k // ring + min(k % ring, ring - k % ring)))
    deep = sorted(range(1, cols), key=lambda k: -(2 * (k // depth) + min(k % depth, depth - k % depth)))
    wide = [2 * k + c for k in far + [0] for c in (0, 1) if 2 * k + c]

    def row_at(k):
        return moved(chip, k // 2, ring) * 2 + lax.rem(core + k % 2, 2)

    def row_back(k):
        return moved_back(chip, k // 2, ring) * 2 + lax.rem(core + k % 2, 2)

    slot_copy = pltpu.make_async_copy(pairs_hbm, pairs_ref, own_sem.at[4])
    slot_copy.start()
    barrier = pltpu.get_barrier_semaphore()
    for k in deep:
        pl.semaphore_signal(barrier, inc=1, device_id=(row, moved(col, k, depth)), device_id_type=MESH)
    for k in wide:
        pl.semaphore_signal(barrier, inc=1, device_id=(row_at(k), col), device_id_type=MESH)
    own = [
        pltpu.make_async_copy(places_ref, tgt_ref.at[pl.ds(row, 1)], own_sem.at[0]),
        pltpu.make_async_copy(places_ref, src_ref.at[pl.ds(col, 1)], own_sem.at[1]),
        pltpu.make_async_copy(omega_ref, omegas_ref.at[pl.ds(col, 1)], own_sem.at[2]),
    ]
    for c in own:
        c.start()
    slot_copy.wait()
    slot_table(cols, pairs_ref, table_ref)
    table = pltpu.make_async_copy(table_ref, meta_ref, own_sem.at[3])
    table.start()
    for h in range(2):
        running_ref[h, slots] = jnp.zeros((rank, half), jnp.float32)
    for c in own:
        c.wait()
    table.wait()
    pl.semaphore_wait(barrier, rows + cols - 2)

    def row_copy(k, slot):
        return pltpu.make_async_remote_copy(
            src_ref=tgt_ref.at[pl.ds(row, 1)], dst_ref=tgt_ref.at[pl.ds(slot, 1)], send_sem=row_send.at[k],
            recv_sem=row_recv.at[k], device_id=(row_at(k), col), device_id_type=MESH)

    def col_copy(k, slot):
        return pltpu.make_async_remote_copy(
            src_ref=src_ref.at[pl.ds(col, 1)], dst_ref=src_ref.at[pl.ds(slot, 1)], send_sem=col_send.at[k],
            recv_sem=col_recv.at[k], device_id=(row, moved(col, k, depth)), device_id_type=MESH)

    def om_copy(k, slot):
        return pltpu.make_async_remote_copy(
            src_ref=omegas_ref.at[pl.ds(col, 1)], dst_ref=omegas_ref.at[pl.ds(slot, 1)], send_sem=om_send.at[k],
            recv_sem=om_recv.at[k], device_id=(row, moved(col, k, depth)), device_id_type=MESH)

    for k in deep:
        col_copy(k, col).start()
    for k in wide:
        row_copy(k, row).start()
    for k in deep:
        om_copy(k, col).start()
    for k in wide:
        row_copy(k, row_back(k)).wait()
    prepare_targets(tgt_ref, feat_ref, centre_ref)
    for k in deep:
        col_copy(k, moved_back(col, k, depth)).wait()
    prepare_sources(src_ref, base_ref, scale_ref)

    def tile_step(i, carry):
        tile_group(i * GROUP, cols, meta_ref, feat_ref, centre_ref, base_ref, scale_ref, tiles_ref)
        return carry

    lax.fori_loop(0, groups, tile_step, 0)
    for k in deep:
        om_copy(k, moved_back(col, k, depth)).wait()

    def pair_copy(h, k):
        return pltpu.make_async_remote_copy(
            src_ref=stage_ref.at[h, k], dst_ref=pair_ref.at[h, k], send_sem=pair_send.at[h, k],
            recv_sem=pair_recv.at[h, k], device_id=(partner, col), device_id_type=MESH)

    def far_copy(h, k):
        return pltpu.make_async_remote_copy(
            src_ref=sum_ref.at[h, k], dst_ref=far_ref.at[h, k], send_sem=far_send.at[h, k],
            recv_sem=far_recv.at[h, k], device_id=(moved(chip, k, ring) * 2 + core, col), device_id_type=MESH)

    for h in range(2):
        def sketch_step(i, carry, h=h):
            sketch_group(i * GROUP, h, cols, meta_ref, omegas_ref, tiles_ref, running_ref)
            return carry

        lax.fori_loop(0, groups, sketch_step, 0)
        for k in far + [0]:
            stage_ref[h, k] = running_ref[h, meta_ref[2, 2 * moved(chip, k, ring) + 1 - core]]
            pair_copy(h, k).start()
        for k in far + [0]:
            sum_ref[h, k] = running_ref[h, meta_ref[2, 2 * moved(chip, k, ring) + core]]
        for k in far + [0]:
            pair_copy(h, k).wait_recv()
            sum_ref[h, k] += pair_ref[h, k]
            if k:
                far_copy(h, k).start()

    totals = []
    for h in range(2):
        total = sum_ref[h, 0]
        for k in reversed(far):
            far_copy(h, k).wait_recv()
            total += far_ref[h, k]
        totals.append(total)

    part = rank // 2

    def out_copy(q, k, slot):
        block = all_ref.at[slot, pl.ds(q * part, part)]
        return pltpu.make_async_remote_copy(
            src_ref=block, dst_ref=block, send_sem=out_send.at[q, k], recv_sem=out_recv.at[q, k],
            device_id=(moved(chip, k, ring) * 2 + core, col), device_id_type=MESH)

    def relay_copy(q, k, slot):
        block = all_ref.at[slot, pl.ds(q * part, part)]
        return pltpu.make_async_remote_copy(
            src_ref=block, dst_ref=block, send_sem=relay_send.at[q, k], recv_sem=relay_recv.at[q, k],
            device_id=(partner, col), device_id_type=MESH)

    def send_part(q):
        block = pl.ds(q * part, part)
        all_ref[row, block] = basis_ref[0, block].astype(jnp.bfloat16)
        for k in far:
            out_copy(q, k, row).start()
        relay_copy(q, 0, row).start()

    factor(jnp.concatenate(totals, axis=1), basis_ref.at[0], lambda: send_part(0))
    send_part(1)
    for h in range(2):
        for k in far:
            pair_copy(h, k).wait_send()
            far_copy(h, k).wait_send()
        pair_copy(h, 0).wait_send()
    for q in range(2):
        for k in reversed(far):
            slot = moved_back(chip, k, ring) * 2 + core
            out_copy(q, k, slot).wait_recv()
            relay_copy(q, k, slot).start()
    for q in range(2):
        for k in far:
            out_copy(q, k, row).wait_send()
        for k in [0] + far[::-1]:
            slot = moved_back(chip, k, ring) * 2 + core
            relay_copy(q, k, slot).wait_send()
            relay_copy(q, k, slot + 1 - 2 * core).wait_recv()


def sketch_and_factor(pairs, places, omega, rows, cols):
    slots = pairs.shape[1]
    rank, n = omega.shape[1], omega.shape[2]
    chips = rows // 2
    bf16, f32 = jnp.bfloat16, jnp.float32
    return pl.pallas_call(
        functools.partial(sketch_kernel, rows, cols),
        out_shape=[
            jax.ShapeDtypeStruct((slots, n, n), bf16),
            jax.ShapeDtypeStruct((1, rank, n), f32),
            jax.ShapeDtypeStruct((rows, rank, n), bf16),
            jax.ShapeDtypeStruct((8, slots), jnp.int32),
        ],
        in_specs=[pl.BlockSpec(memory_space=pltpu.HBM)] * 3,
        out_specs=[pl.BlockSpec(memory_space=VMEM)] * 4,
        scratch_shapes=[
            VMEM((2, slots), jnp.int32), SMEM((8, slots), jnp.int32),
            VMEM((rows,) + places.shape[1:], f32), VMEM((cols,) + places.shape[1:], f32),
            VMEM((cols, rank, n), bf16),
            VMEM((rows, n, 48), bf16), VMEM((rows, 8, n), f32),
            VMEM((cols, 8, n), f32), VMEM((cols, 8, n), f32),
            VMEM((2, slots + 1, rank, n // 2), f32),
            VMEM((2, chips, rank, n // 2), f32), VMEM((2, chips, rank, n // 2), f32),
            VMEM((2, chips, rank, n // 2), f32), VMEM((2, chips, rank, n // 2), f32),
            DMA((5,)), DMA((rows,)), DMA((rows,)), DMA((cols,)), DMA((cols,)), DMA((cols,)), DMA((cols,)),
            DMA((2, chips)), DMA((2, chips)), DMA((2, chips)), DMA((2, chips)),
            DMA((2, chips)), DMA((2, chips)), DMA((2, chips)), DMA((2, chips)),
        ],
        compiler_params=pltpu.CompilerParams(collective_id=0, has_side_effects=True,
                                             vmem_limit_bytes=24 << 20),
        name="sketch_and_factor",
    )(*(pltpu.with_memory_space_constraint(x, pltpu.HBM) for x in (pairs, places, omega)))


def project_kernel(cols, meta_ref, basis_all_ref, basis_ref, tiles_ref, out_hbm, bases_ref, out_ref, out_sem):
    slots, n = tiles_ref.shape[0], tiles_ref.shape[1]
    groups = slots // GROUP

    def out_copy(i):
        part = pl.ds(i * GROUP, GROUP)
        return pltpu.make_async_copy(out_ref.at[part], out_hbm.at[part], out_sem.at[i])

    def step(i, carry):
        for g in range(GROUP):
            p = i * GROUP + g
            live = meta_ref[3, p].astype(jnp.float32)
            result = jnp.dot(basis_all_ref[meta_ref[0, p] // cols], tiles_ref[p],
                             preferred_element_type=jnp.float32)
            out_ref[p] = (result * live).astype(jnp.bfloat16)
        out_copy(i).start()
        return carry

    def finish(i, carry):
        out_copy(i).wait()
        return carry

    lax.fori_loop(0, groups, step, 0)
    bases_ref[...] = basis_ref[...] * math.sqrt(n)
    lax.fori_loop(0, groups, finish, 0)


def project(meta, tiles, basis, basis_all, cols):
    slots = tiles.shape[0]
    rank, n = basis_all.shape[1], basis_all.shape[2]
    return pl.pallas_call(
        functools.partial(project_kernel, cols),
        out_shape=[
            jax.ShapeDtypeStruct((slots, rank, n), jnp.bfloat16),
            jax.ShapeDtypeStruct(basis.shape, basis.dtype),
        ],
        in_specs=[pl.BlockSpec(memory_space=SMEM)] + [pl.BlockSpec(memory_space=VMEM)] * 3,
        out_specs=[pl.BlockSpec(memory_space=pl.ANY), pl.BlockSpec(memory_space=VMEM)],
        scratch_shapes=[VMEM((slots, rank, n), jnp.bfloat16), DMA((slots // GROUP,))],
        compiler_params=pltpu.CompilerParams(vmem_limit_bytes=12 << 20),
        name="project",
    )(meta, basis_all, basis, tiles)


def body(places, omega, pairs):
    rows, cols = lax.axis_size("row"), lax.axis_size("col")
    pairs = pairs.T
    tiles, basis, basis_all, meta = sketch_and_factor(pairs, places, omega, rows, cols)
    coeffs, bases = project(meta, tiles, basis, basis_all, cols)
    return (bases, coeffs)


def solution(mesh):
    in_specs = (
        P(("row", "col"), None, None),
        P(("row", "col"), None, None),
        P(("row", "col"), None),
    )
    out_specs = (P(("row", "col"), None, None), P(("row", "col"), None, None))
    return jax.shard_map(body, mesh=mesh, in_specs=in_specs, out_specs=out_specs, check_vma=False)
```

time: 65.3 us -> 57 us (0.87)
  Pallas kernels: 63.7 us -> 56.2 us
    pallas_call x2 -> x1, Pallas kernels: 10.7 us -> 6.12 us  [project(): pl.pallas_call(functools.partial(project_kernel, cols), out_shape=[jax.Sh...]
    pallas_call x1, Pallas kernels: 53 us -> 50 us  [sketch_and_factor(): pl.pallas_call(functools.partial(sketch_kernel, rows, cols), out_shape=[j...]
where the time goes in v3:
time: 57 us; the launch traced here: 56.8 us
  Pallas kernels  56.2 us (99%)
  between operations  0.64 us (1%)
    pallas_call x1, Pallas kernels, sketch_and_factor(): pl.pallas_call(functools.partial(sketch_kernel, rows, cols), out_shape=[j...  50 us
    pallas_call x1, Pallas kernels, project(): pl.pallas_call(functools.partial(project_kernel, cols), out_shape=[jax.Sh...  6.12 us

profile of v3, /device:TPU:1, one launch (start us, length us, event | category | flops | bytes accessed | tf_op | source)
XLA Modules:
  0.0 56.8 jit_solution(12384768345765210376)
XLA Ops:
  0.6 50.0 %sketch_and_factor.1 = (bf16[128,256,256]{2,1,0:T(8,128)(2,1)S(1)}, f32[1,64,256]{2,1,0:T(8,128)S(1)}, bf16[16,64,256]{2,1,0:T(8,128)(2,1)S(1)}, s32[8,128]{1,0:T(8,128)S(1)}) custom-call(s32[2,128]{1,0:T(2,128)} %bitcast.1, f32[1,4,256]{2,1,0:T(4,128)} %places_ref.1, bf16[1,64,256]{2,1,0:T(8,128)(2,1)} %omega_ref.1), custom_call_target="tpu_custom_call" | custom-call | tf_op jit(solution)/shard_map/sketch_and_factor/pallas_call | solution.py:327
  50.7 6.1 %project.1 = (bf16[128,64,256]{2,1,0:T(8,128)(2,1)}, f32[1,64,256]{2,1,0:T(8,128)}) custom-call(s32[8,128]{1,0:T(8,128)S(1)} %get-tuple-element.8.meta_ref, bf16[16,64,256]{2,1,0:T(8,128)(2,1)S(1)} %get-tuple-element.9.basis_all_ref, f32[1,64,256]{2,1,0:T(8,128)S(1)} %get-tuple-element.10.basis_ref, bf16[128,256,256]{2,1,0:T(8,128)(2,1)S(1)} %get-tuple-element.11.tiles_ref), custom_call_target="tpu_custom_call" | custom-call | tf_op jit(solution)/shard_map/project/pallas_call | solution.py:386

commit v4 on v3

--- a/solution.py
+++ b/solution.py
@@ -14,7 +14,7 @@
 VMEM = pltpu.VMEM
 SMEM = pltpu.SMEM
 DMA = pltpu.SemaphoreType.DMA
-GROUP = 16
+GROUP = 32
 NT = (((1,), (1,)), ((), ()))
 
 
@@ -122,31 +122,39 @@
         running_ref[h, first + g] = running_ref[h, meta_ref[1, first + g]] + parts[g]
 
 
-def factor(sketch, out, at_half):
+def gram_of(sketch):
+    return lax.dot_general(sketch, sketch, NT, precision=lax.Precision.HIGHEST,
+                           preferred_element_type=jnp.float32)
+
+
+def energy_of(sketch):
+    return jnp.sum(jnp.sum(sketch * sketch, axis=0, keepdims=True), axis=1, keepdims=True)
+
+
+def factor(sketch, gram, energy, out, at_half):
     rank, width = sketch.shape
-    gram = lax.dot_general(sketch, sketch, NT, precision=lax.Precision.HIGHEST,
-                           preferred_element_type=jnp.float32)
-    energy = jnp.sum(jnp.sum(sketch * sketch, axis=0, keepdims=True), axis=1, keepdims=True)
     shift = ridge * energy / rank
     eye = (lax.broadcasted_iota(jnp.int32, (rank, rank), 0)
            == lax.broadcasted_iota(jnp.int32, (rank, rank), 1))
     mat = gram + jnp.where(eye, shift, 0.0)
+
+    def wide(x):
+        return jnp.concatenate([x] * (width // 128), axis=1)
+
     for b in range(0, rank, 8):
         rows = rank - b
         row_at = lax.broadcasted_iota(jnp.int32, (rows, 1), 0)
         columns = [jnp.broadcast_to(mat[:, b + j:b + j + 1], (rows, 128)) for j in range(8)]
         for k in range(8):
-            inv = lax.rsqrt(columns[k][k:k + 1, :])
-            inv_wide = jnp.concatenate([inv] * (width // 128), axis=1)
+            inv = lax.rsqrt(columns[k][k:k + 1])
             mult = jnp.where(row_at > k, columns[k] * inv, 0.0)
-            mult_wide = jnp.concatenate([mult] * (width // 128), axis=1)
-            mat_row = mat[k:k + 1, :] * inv[:, :rank]
-            sketch_row = sketch[k:k + 1, :] * inv_wide
+            mat_row = mat[k:k + 1] * inv[:, :rank]
+            sketch_row = sketch[k:k + 1] * wide(inv)
             out[b + k:b + k + 1, :] = sketch_row
             for j in range(k + 1, 8):
-                columns[j] = columns[j] - mult * (columns[j][k:k + 1, :] * inv)
+                columns[j] = columns[j] - mult * (columns[j][k:k + 1] * inv)
             mat = mat - mult[:, :rank] * mat_row
-            sketch = sketch - mult_wide * sketch_row
+            sketch = sketch - wide(mult) * sketch_row
         mat, sketch = mat[8:], sketch[8:]
         if 2 * (b + 8) == rank:
             at_half()
@@ -203,7 +211,6 @@
         running_ref[h, slots] = jnp.zeros((rank, half), jnp.float32)
     for c in own:
         c.wait()
-    table.wait()
     pl.semaphore_wait(barrier, rows + cols - 2)
 
     def row_copy(k, slot):
@@ -221,11 +228,26 @@
             src_ref=omegas_ref.at[pl.ds(col, 1)], dst_ref=omegas_ref.at[pl.ds(slot, 1)], send_sem=om_send.at[k],
             recv_sem=om_recv.at[k], device_id=(row, moved(col, k, depth)), device_id_type=MESH)
 
-    for k in deep:
+    def om_relay(k, slot):
+        return pltpu.make_async_remote_copy(
+            src_ref=omegas_ref.at[pl.ds(slot, 1)], dst_ref=omegas_ref.at[pl.ds(slot, 1)],
+            send_sem=om_send.at[depth + k], recv_sem=om_recv.at[depth + k],
+            device_id=(row, moved(col, depth, depth)), device_id_type=MESH)
+
+    def hand_on(ks):
+        for k in ks:
+            om_copy(k, moved_back(col, k, depth)).wait_recv()
+            om_relay(k, moved_back(col, k, depth)).start()
+
+    near = sorted(range(1, depth), key=lambda k: min(k, depth - k))
+    for k in deep[:cols // 2]:
+        col_copy(k, col).start()
+    for k in deep[cols // 2:]:
         col_copy(k, col).start()
     for k in wide:
         row_copy(k, row).start()
-    for k in deep:
+    om_relay(0, col).start()
+    for k in near:
         om_copy(k, col).start()
     for k in wide:
         row_copy(k, row_back(k)).wait()
@@ -233,19 +255,35 @@
     for k in deep:
         col_copy(k, moved_back(col, k, depth)).wait()
     prepare_sources(src_ref, base_ref, scale_ref)
+    table.wait()
+    cut = len(near) // 2 + 1
+    hand_on(near[:cut])
 
     def tile_step(i, carry):
         tile_group(i * GROUP, cols, meta_ref, feat_ref, centre_ref, base_ref, scale_ref, tiles_ref)
+
+        @pl.when(i == 0)
+        def _():
+            hand_on(near[cut:-1])
+
+        @pl.when(i == 1)
+        def _():
+            hand_on(near[-1:])
+
         return carry
 
     lax.fori_loop(0, groups, tile_step, 0)
-    for k in deep:
-        om_copy(k, moved_back(col, k, depth)).wait()
-
-    def pair_copy(h, k):
-        return pltpu.make_async_remote_copy(
-            src_ref=stage_ref.at[h, k], dst_ref=pair_ref.at[h, k], send_sem=pair_send.at[h, k],
-            recv_sem=pair_recv.at[h, k], device_id=(partner, col), device_id_type=MESH)
+    for k in near:
+        om_copy(k, col).wait_send()
+    for k in [0] + near:
+        om_relay(k, col).wait_send()
+        om_relay(k, col).wait_recv()
+
+    def pair_copy(h, q):
+        block = pl.ds(q * ring, ring)
+        return pltpu.make_async_remote_copy(
+            src_ref=stage_ref.at[h, block], dst_ref=pair_ref.at[h, block], send_sem=pair_send.at[h, q],
+            recv_sem=pair_recv.at[h, q], device_id=(partner, col), device_id_type=MESH)
 
     def far_copy(h, k):
         return pltpu.make_async_remote_copy(
@@ -258,23 +296,27 @@
             return carry
 
         lax.fori_loop(0, groups, sketch_step, 0)
-        for k in far + [0]:
-            stage_ref[h, k] = running_ref[h, meta_ref[2, 2 * moved(chip, k, ring) + 1 - core]]
-            pair_copy(h, k).start()
-        for k in far + [0]:
+        for q in (1, 0):
+            for k in range(q * ring, (q + 1) * ring):
+                stage_ref[h, k] = running_ref[h, meta_ref[2, 2 * moved(chip, k, ring) + 1 - core]]
+            pair_copy(h, q).start()
+        for k in range(chips):
             sum_ref[h, k] = running_ref[h, meta_ref[2, 2 * moved(chip, k, ring) + core]]
-        for k in far + [0]:
-            pair_copy(h, k).wait_recv()
-            sum_ref[h, k] += pair_ref[h, k]
-            if k:
+        for q in (1, 0):
+            pair_copy(h, q).wait_recv()
+            for k in [k for k in far if k // ring == q]:
+                sum_ref[h, k] += pair_ref[h, k]
                 far_copy(h, k).start()
-
-    totals = []
+        sum_ref[h, 0] += pair_ref[h, 0]
+
+    totals, gram, energy = [], None, None
     for h in range(2):
         total = sum_ref[h, 0]
         for k in reversed(far):
             far_copy(h, k).wait_recv()
             total += far_ref[h, k]
+        gram = gram_of(total) if h == 0 else gram + gram_of(total)
+        energy = energy_of(total) if h == 0 else energy + energy_of(total)
         totals.append(total)
 
     part = rank // 2
@@ -298,13 +340,13 @@
             out_copy(q, k, row).start()
         relay_copy(q, 0, row).start()
 
-    factor(jnp.concatenate(totals, axis=1), basis_ref.at[0], lambda: send_part(0))
+    factor(jnp.concatenate(totals, axis=1), gram, energy, basis_ref.at[0], lambda: send_part(0))
     send_part(1)
     for h in range(2):
         for k in far:
-            pair_copy(h, k).wait_send()
             far_copy(h, k).wait_send()
-        pair_copy(h, 0).wait_send()
+        for q in range(2):
+            pair_copy(h, q).wait_send()
     for q in range(2):
         for k in reversed(far):
             slot = moved_back(chip, k, ring) * 2 + core
@@ -344,7 +386,7 @@
             VMEM((2, chips, rank, n // 2), f32), VMEM((2, chips, rank, n // 2), f32),
             VMEM((2, chips, rank, n // 2), f32), VMEM((2, chips, rank, n // 2), f32),
             DMA((5,)), DMA((rows,)), DMA((rows,)), DMA((cols,)), DMA((cols,)), DMA((cols,)), DMA((cols,)),
-            DMA((2, chips)), DMA((2, chips)), DMA((2, chips)), DMA((2, chips)),
+            DMA((2, 2)), DMA((2, 2)), DMA((2, chips)), DMA((2, chips)),
             DMA((2, chips)), DMA((2, chips)), DMA((2, chips)), DMA((2, chips)),
         ],
         compiler_params=pltpu.CompilerParams(collective_id=0, has_side_effects=True,

time: 57 us -> 54.7 us (0.960)
  Pallas kernels: 56.2 us -> 53.9 us
    pallas_call x1, Pallas kernels: 50 us -> 48.1 us  [sketch_and_factor(): pl.pallas_call(functools.partial(sketch_kernel, rows, cols), out_shape=[j...]
where the time goes in v4:
time: 54.7 us; the launch traced here: 54.6 us
  Pallas kernels  53.9 us (99%)
  between operations  0.64 us (1%)
    pallas_call x1, Pallas kernels, sketch_and_factor(): pl.pallas_call(functools.partial(sketch_kernel, rows, cols), out_shape=[j...  48.1 us
    pallas_call x1, Pallas kernels, project(): pl.pallas_call(functools.partial(project_kernel, cols), out_shape=[jax.Sh...  5.83 us

profile of v4, /device:TPU:1, one launch (start us, length us, event | category | flops | bytes accessed | tf_op | source)
XLA Modules:
  0.0 54.6 jit_solution(14161441405210338854)
XLA Ops:
  0.6 48.1 %sketch_and_factor.1 = (bf16[128,256,256]{2,1,0:T(8,128)(2,1)S(1)}, f32[1,64,256]{2,1,0:T(8,128)S(1)}, bf16[16,64,256]{2,1,0:T(8,128)(2,1)S(1)}, s32[8,128]{1,0:T(8,128)S(1)}) custom-call(s32[2,128]{1,0:T(2,128)} %bitcast.1, f32[1,4,256]{2,1,0:T(4,128)} %places_ref.1, bf16[1,64,256]{2,1,0:T(8,128)(2,1)} %omega_ref.1), custom_call_target="tpu_custom_call" | custom-call | tf_op jit(solution)/shard_map/sketch_and_factor/pallas_call | solution.py:369
  48.7 5.8 %project.1 = (bf16[128,64,256]{2,1,0:T(8,128)(2,1)}, f32[1,64,256]{2,1,0:T(8,128)}) custom-call(s32[8,128]{1,0:T(8,128)S(1)} %get-tuple-element.8.meta_ref, bf16[16,64,256]{2,1,0:T(8,128)(2,1)S(1)} %get-tuple-element.9.basis_all_ref, f32[1,64,256]{2,1,0:T(8,128)S(1)} %get-tuple-element.10.basis_ref, bf16[128,256,256]{2,1,0:T(8,128)(2,1)S(1)} %get-tuple-element.11.tiles_ref), custom_call_target="tpu_custom_call" | custom-call | tf_op jit(solution)/shard_map/project/pallas_call | solution.py:428

commit v5 on v4

--- a/solution.py
+++ b/solution.py
@@ -52,19 +52,21 @@
     return hi, mid, rest - mid
 
 
-def target_features(spots, row8):
-    n = spots.shape[1]
-    coords = jnp.concatenate([spots[0:3], jnp.zeros((5, n), jnp.float32)], axis=0)
-    centre = jnp.sum(coords, axis=1, keepdims=True) * (1.0 / n)
-    moved = coords - centre
+def coords_of(spots):
+    return jnp.concatenate([spots[0:3], jnp.zeros((5, spots.shape[1]), jnp.float32)], axis=0)
+
+
+def streamed(base, scale, row8):
+    centre = jnp.sum(base, axis=1, keepdims=True) * (1.0 / base.shape[1])
+    moved = base - centre
     norm = jnp.sum(moved * moved, axis=0, keepdims=True) + soft_sq
-    feats = jnp.where(row8 == 3, norm, jnp.where(row8 == 4, 1.0, -2.0 * moved))
+    feats = scale * jnp.where(row8 == 3, norm, jnp.where(row8 == 4, 1.0, -2.0 * moved))
     hi, mid, low = split(feats)
     stack = jnp.concatenate([hi, mid, low, hi, mid, hi], axis=0)
-    return stack.T.astype(jnp.bfloat16), centre
-
-
-def source_features(base, scale, centre, row8):
+    return stack.T.astype(jnp.bfloat16), jnp.broadcast_to(centre, base.shape)
+
+
+def held(base, scale, centre, row8):
     moved = base - centre
     norm = jnp.sum(moved * moved, axis=0, keepdims=True)
     feats = scale * jnp.where(row8 == 3, 1.0, jnp.where(row8 == 4, norm, moved))
@@ -72,51 +74,65 @@
     return jnp.concatenate([hi, hi, hi, mid, mid, low], axis=0).astype(jnp.bfloat16)
 
 
-def prepare_targets(tgt_ref, feat_ref, centre_ref):
+def prepare_targets(tgt_ref, base_ref, feat_ref, centre_ref):
     n = tgt_ref.shape[2]
     row8 = lax.broadcasted_iota(jnp.int32, (8, n), 0)
 
     def one(t, carry):
-        feats, centre = target_features(tgt_ref[t], row8)
-        feat_ref[t] = feats
-        centre_ref[t] = jnp.broadcast_to(centre, (8, n))
+        base = coords_of(tgt_ref[t])
+        base_ref[t] = base
+        feat_ref[t], centre_ref[t] = streamed(base, 1.0, row8)
         return carry
 
     lax.fori_loop(0, tgt_ref.shape[0], one, 0, unroll=4)
 
 
-def prepare_sources(src_ref, base_ref, scale_ref):
+def prepare_sources(src_ref, base_ref, scale_ref, feat_ref, centre_ref):
     n = src_ref.shape[2]
+    row8 = lax.broadcasted_iota(jnp.int32, (8, n), 0)
 
     def one(s, carry):
         spots = src_ref[s]
-        base_ref[s] = jnp.concatenate([spots[0:3], jnp.zeros((5, n), jnp.float32)], axis=0)
+        base = coords_of(spots)
         weight = spots[3:4]
-        scale_ref[s] = jnp.broadcast_to(1.0 / (weight * weight), (8, n))
+        scale = jnp.broadcast_to(1.0 / (weight * weight), (8, n))
+        base_ref[s], scale_ref[s] = base, scale
+        feat_ref[s], centre_ref[s] = streamed(base, scale, row8)
         return carry
 
     lax.fori_loop(0, src_ref.shape[0], one, 0, unroll=4)
 
 
-def tile_group(first, cols, meta_ref, feat_ref, centre_ref, base_ref, scale_ref, tiles_ref):
-    n = feat_ref.shape[1]
+def turned_group(first, cols, meta_ref, tgt_base, src_feat, src_centre, turned_ref):
+    n = src_feat.shape[1]
     row8 = lax.broadcasted_iota(jnp.int32, (8, n), 0)
     for g in range(GROUP):
         code = meta_ref[0, first + g]
         t, s = code // cols, code % cols
-        source = source_features(base_ref[s], scale_ref[s], centre_ref[t], row8)
-        dist = jnp.dot(feat_ref[t], source, preferred_element_type=jnp.float32)
+        target = held(tgt_base[t], 1.0, src_centre[s], row8)
+        dist = jnp.dot(src_feat[s], target, preferred_element_type=jnp.float32)
+        turned_ref[first + g] = lax.rsqrt(dist).astype(jnp.bfloat16)
+
+
+def tile_group(first, cols, meta_ref, src_base, src_scale, tgt_feat, tgt_centre, tiles_ref):
+    n = tgt_feat.shape[1]
+    row8 = lax.broadcasted_iota(jnp.int32, (8, n), 0)
+    for g in range(GROUP):
+        code = meta_ref[0, first + g]
+        t, s = code // cols, code % cols
+        source = held(src_base[s], src_scale[s], tgt_centre[t], row8)
+        dist = jnp.dot(tgt_feat[t], source, preferred_element_type=jnp.float32)
         tiles_ref[first + g] = lax.rsqrt(dist).astype(jnp.bfloat16)
 
 
-def sketch_group(first, h, cols, meta_ref, omegas_ref, tiles_ref, running_ref):
+def sketch_group(first, h, cols, meta_ref, omegas_ref, turned_ref, running_ref):
     half = running_ref.shape[3]
     parts = []
     for g in range(GROUP):
         s = meta_ref[0, first + g] % cols
         live = meta_ref[3, first + g].astype(jnp.float32)
-        part = lax.dot_general(omegas_ref[s], tiles_ref[first + g, h * half:(h + 1) * half], NT,
-                               preferred_element_type=jnp.float32)
+        part = jnp.dot(omegas_ref[s], turned_ref[first + g, :, h * half:(h + 1) * half],
+                       preferred_element_type=jnp.float32)
         parts.append(part * live)
     for g in range(GROUP):
         running_ref[h, first + g] = running_ref[h, meta_ref[1, first + g]] + parts[g]
@@ -161,8 +177,8 @@
 
 
 def sketch_kernel(rows, cols, pairs_hbm, places_ref, omega_ref, tiles_ref, basis_ref, all_ref, table_ref,
-                  pairs_ref, meta_ref, tgt_ref, src_ref, omegas_ref, feat_ref, centre_ref, base_ref, scale_ref,
-                  running_ref, stage_ref, pair_ref, sum_ref, far_ref,
+                  pairs_ref, meta_ref, tgt_ref, src_ref, omegas_ref, tgt_base, tgt_feat, tgt_centre,
+                  src_base, src_scale, src_feat, src_centre, turned_ref, running_ref, stage_ref, pair_ref, sum_ref, far_ref,
                   own_sem, row_send, row_recv, col_send, col_recv, om_send, om_recv,
                   pair_send, pair_recv, far_send, far_recv, out_send, out_recv, relay_send, relay_recv):
     row, col = lax.axis_index("row"), lax.axis_index("col")
@@ -251,16 +267,16 @@
         om_copy(k, col).start()
     for k in wide:
         row_copy(k, row_back(k)).wait()
-    prepare_targets(tgt_ref, feat_ref, centre_ref)
+    prepare_targets(tgt_ref, tgt_base, tgt_feat, tgt_centre)
     for k in deep:
         col_copy(k, moved_back(col, k, depth)).wait()
-    prepare_sources(src_ref, base_ref, scale_ref)
+    prepare_sources(src_ref, src_base, src_scale, src_feat, src_centre)
     table.wait()
     cut = len(near) // 2 + 1
     hand_on(near[:cut])
 
-    def tile_step(i, carry):
-        tile_group(i * GROUP, cols, meta_ref, feat_ref, centre_ref, base_ref, scale_ref, tiles_ref)
+    def turned_step(i, carry):
+        turned_group(i * GROUP, cols, meta_ref, tgt_base, src_feat, src_centre, turned_ref)
 
         @pl.when(i == 0)
         def _():
@@ -272,7 +288,7 @@
 
         return carry
 
-    lax.fori_loop(0, groups, tile_step, 0)
+    lax.fori_loop(0, groups, turned_step, 0)
     for k in near:
         om_copy(k, col).wait_send()
     for k in [0] + near:
@@ -290,24 +306,48 @@
             src_ref=sum_ref.at[h, k], dst_ref=far_ref.at[h, k], send_sem=far_send.at[h, k],
             recv_sem=far_recv.at[h, k], device_id=(moved(chip, k, ring) * 2 + core, col), device_id_type=MESH)
 
-    for h in range(2):
-        def sketch_step(i, carry, h=h):
-            sketch_group(i * GROUP, h, cols, meta_ref, omegas_ref, tiles_ref, running_ref)
-            return carry
-
-        lax.fori_loop(0, groups, sketch_step, 0)
+    def swap(h):
         for q in (1, 0):
             for k in range(q * ring, (q + 1) * ring):
                 stage_ref[h, k] = running_ref[h, meta_ref[2, 2 * moved(chip, k, ring) + 1 - core]]
             pair_copy(h, q).start()
         for k in range(chips):
             sum_ref[h, k] = running_ref[h, meta_ref[2, 2 * moved(chip, k, ring) + core]]
+
+    def send_sums(h):
         for q in (1, 0):
             pair_copy(h, q).wait_recv()
             for k in [k for k in far if k // ring == q]:
                 sum_ref[h, k] += pair_ref[h, k]
                 far_copy(h, k).start()
         sum_ref[h, 0] += pair_ref[h, 0]
+
+    def first_half(i, carry):
+        sketch_group(i * GROUP, 0, cols, meta_ref, omegas_ref, turned_ref, running_ref)
+        return carry
+
+    def second_half(i, carry):
+        @pl.when(i == groups // 2)
+        def _():
+            send_sums(0)
+
+        sketch_group(i * GROUP, 1, cols, meta_ref, omegas_ref, turned_ref, running_ref)
+        return carry
+
+    lax.fori_loop(0, groups, first_half, 0)
+    swap(0)
+    lax.fori_loop(0, groups, second_half, 0)
+    swap(1)
+
+    def tile_step(i, carry):
+        @pl.when(i == 1)
+        def _():
+            send_sums(1)
+
+        tile_group(i * GROUP, cols, meta_ref, src_base, src_scale, tgt_feat, tgt_centre, tiles_ref)
+        return carry
+
+    lax.fori_loop(0, groups, tile_step, 0)
 
     totals, gram, energy = [], None, None
     for h in range(2):
@@ -380,8 +420,9 @@
             VMEM((2, slots), jnp.int32), SMEM((8, slots), jnp.int32),
             VMEM((rows,) + places.shape[1:], f32), VMEM((cols,) + places.shape[1:], f32),
             VMEM((cols, rank, n), bf16),
-            VMEM((rows, n, 48), bf16), VMEM((rows, 8, n), f32),
-            VMEM((cols, 8, n), f32), VMEM((cols, 8, n), f32),
+            VMEM((rows, 8, n), f32), VMEM((rows, n, 48), bf16), VMEM((rows, 8, n), f32),
+            VMEM((cols, 8, n), f32), VMEM((cols, 8, n), f32), VMEM((cols, n, 48), bf16), VMEM((cols, 8, n), f32),
+            VMEM((slots, n, n), bf16),
             VMEM((2, slots + 1, rank, n // 2), f32),
             VMEM((2, chips, rank, n // 2), f32), VMEM((2, chips, rank, n // 2), f32),
             VMEM((2, chips, rank, n // 2), f32), VMEM((2, chips, rank, n // 2), f32),
@@ -390,7 +431,7 @@
             DMA((2, chips)), DMA((2, chips)), DMA((2, chips)), DMA((2, chips)),
         ],
         compiler_params=pltpu.CompilerParams(collective_id=0, has_side_effects=True,
-                                             vmem_limit_bytes=24 << 20),
+                                             vmem_limit_bytes=36 << 20),
         name="sketch_and_factor",
     )(*(pltpu.with_memory_space_constraint(x, pltpu.HBM) for x in (pairs, places, omega)))
 

time: 54.7 us -> 52.5 us (0.960)
  Pallas kernels: 53.9 us -> 51.7 us
    pallas_call x1, Pallas kernels: 48.1 us -> 46 us  [sketch_and_factor(): pl.pallas_call(functools.partial(sketch_kernel, rows, cols), out_shape=[j...]
where the time goes in v5:
time: 52.5 us; the launch traced here: 52.3 us
  Pallas kernels  51.7 us (98%)
  between operations  0.64 us (1%)
    pallas_call x1, Pallas kernels, sketch_and_factor(): pl.pallas_call(functools.partial(sketch_kernel, rows, cols), out_shape=[j...  46 us
    pallas_call x1, Pallas kernels, project(): pl.pallas_call(functools.partial(project_kernel, cols), out_shape=[jax.Sh...  5.64 us

profile of v5, /device:TPU:1, one launch (start us, length us, event | category | flops | bytes accessed | tf_op | source)
XLA Modules:
  0.0 52.3 jit_solution(6410793996611573160)
XLA Ops:
  0.6 46.0 %sketch_and_factor.1 = (bf16[128,256,256]{2,1,0:T(8,128)(2,1)S(1)}, f32[1,64,256]{2,1,0:T(8,128)S(1)}, bf16[16,64,256]{2,1,0:T(8,128)(2,1)S(1)}, s32[8,128]{1,0:T(8,128)S(1)}) custom-call(s32[2,128]{1,0:T(2,128)} %bitcast.1, f32[1,4,256]{2,1,0:T(4,128)} %places_ref.1, bf16[1,64,256]{2,1,0:T(8,128)(2,1)} %omega_ref.1), custom_call_target="tpu_custom_call" | custom-call | tf_op jit(solution)/shard_map/sketch_and_factor/pallas_call | solution.py:409
  46.7 5.6 %project.1 = (bf16[128,64,256]{2,1,0:T(8,128)(2,1)}, f32[1,64,256]{2,1,0:T(8,128)}) custom-call(s32[8,128]{1,0:T(8,128)S(1)} %get-tuple-element.8.meta_ref, bf16[16,64,256]{2,1,0:T(8,128)(2,1)S(1)} %get-tuple-element.9.basis_all_ref, f32[1,64,256]{2,1,0:T(8,128)S(1)} %get-tuple-element.10.basis_ref, bf16[128,256,256]{2,1,0:T(8,128)(2,1)S(1)} %get-tuple-element.11.tiles_ref), custom_call_target="tpu_custom_call" | custom-call | tf_op jit(solution)/shard_map/project/pallas_call | solution.py:469

commit v6 on v5

--- a/solution.py
+++ b/solution.py
@@ -15,6 +15,8 @@
 SMEM = pltpu.SMEM
 DMA = pltpu.SemaphoreType.DMA
 GROUP = 32
+LONG = 64
+PIECE = 16
 NT = (((1,), (1,)), ((), ()))
 
 
@@ -327,7 +329,7 @@
         return carry
 
     def second_half(i, carry):
-        @pl.when(i == groups // 2)
+        @pl.when(i == groups - 1)
         def _():
             send_sums(0)
 
@@ -438,29 +440,29 @@
 
 def project_kernel(cols, meta_ref, basis_all_ref, basis_ref, tiles_ref, out_hbm, bases_ref, out_ref, out_sem):
     slots, n = tiles_ref.shape[0], tiles_ref.shape[1]
-    groups = slots // GROUP
 
     def out_copy(i):
-        part = pl.ds(i * GROUP, GROUP)
+        part = pl.ds(i * PIECE, PIECE)
         return pltpu.make_async_copy(out_ref.at[part], out_hbm.at[part], out_sem.at[i])
 
     def step(i, carry):
-        for g in range(GROUP):
-            p = i * GROUP + g
+        for g in range(LONG):
+            p = i * LONG + g
             live = meta_ref[3, p].astype(jnp.float32)
             result = jnp.dot(basis_all_ref[meta_ref[0, p] // cols], tiles_ref[p],
                              preferred_element_type=jnp.float32)
             out_ref[p] = (result * live).astype(jnp.bfloat16)
-        out_copy(i).start()
+            if (g + 1) % PIECE == 0:
+                out_copy(i * (LONG // PIECE) + g // PIECE).start()
         return carry
 
     def finish(i, carry):
         out_copy(i).wait()
         return carry
 
-    lax.fori_loop(0, groups, step, 0)
+    lax.fori_loop(0, slots // LONG, step, 0)
     bases_ref[...] = basis_ref[...] * math.sqrt(n)
-    lax.fori_loop(0, groups, finish, 0)
+    lax.fori_loop(0, slots // PIECE, finish, 0)
 
 
 def project(meta, tiles, basis, basis_all, cols):
@@ -474,7 +476,7 @@
         ],
         in_specs=[pl.BlockSpec(memory_space=SMEM)] + [pl.BlockSpec(memory_space=VMEM)] * 3,
         out_specs=[pl.BlockSpec(memory_space=pl.ANY), pl.BlockSpec(memory_space=VMEM)],
-        scratch_shapes=[VMEM((slots, rank, n), jnp.bfloat16), DMA((slots // GROUP,))],
+        scratch_shapes=[VMEM((slots, rank, n), jnp.bfloat16), DMA((slots // PIECE,))],
         compiler_params=pltpu.CompilerParams(vmem_limit_bytes=12 << 20),
         name="project",
     )(meta, basis_all, basis, tiles)

time: 52.5 us -> 51.7 us (0.985)
  Pallas kernels: 51.7 us -> 50.9 us
where the time goes in v6:
time: 51.7 us; the launch traced here: 51.5 us
  Pallas kernels  50.9 us (98%)
  between operations  0.64 us (1%)
    pallas_call x1, Pallas kernels, sketch_and_factor(): pl.pallas_call(functools.partial(sketch_kernel, rows, cols), out_shape=[j...  45.7 us
    pallas_call x1, Pallas kernels, project(): pl.pallas_call(functools.partial(project_kernel, cols), out_shape=[jax.Sh...  5.24 us

profile of v6, /device:TPU:1, one launch (start us, length us, event | category | flops | bytes accessed | tf_op | source)
XLA Modules:
  0.0 51.5 jit_solution(14371825088587472749)
XLA Ops:
  0.6 45.7 %sketch_and_factor.1 = (bf16[128,256,256]{2,1,0:T(8,128)(2,1)S(1)}, f32[1,64,256]{2,1,0:T(8,128)S(1)}, bf16[16,64,256]{2,1,0:T(8,128)(2,1)S(1)}, s32[8,128]{1,0:T(8,128)S(1)}) custom-call(s32[2,128]{1,0:T(2,128)} %bitcast.1, f32[1,4,256]{2,1,0:T(4,128)} %places_ref.1, bf16[1,64,256]{2,1,0:T(8,128)(2,1)} %omega_ref.1), custom_call_target="tpu_custom_call" | custom-call | tf_op jit(solution)/shard_map/sketch_and_factor/pallas_call | solution.py:411
  46.3 5.2 %project.1 = (bf16[128,64,256]{2,1,0:T(8,128)(2,1)}, f32[1,64,256]{2,1,0:T(8,128)}) custom-call(s32[8,128]{1,0:T(8,128)S(1)} %get-tuple-element.8.meta_ref, bf16[16,64,256]{2,1,0:T(8,128)(2,1)S(1)} %get-tuple-element.9.basis_all_ref, f32[1,64,256]{2,1,0:T(8,128)S(1)} %get-tuple-element.10.basis_ref, bf16[128,256,256]{2,1,0:T(8,128)(2,1)S(1)} %get-tuple-element.11.tiles_ref), custom_call_target="tpu_custom_call" | custom-call | tf_op jit(solution)/shard_map/project/pallas_call | solution.py:471

commit v7 on v6

--- a/solution.py
+++ b/solution.py
@@ -130,13 +130,13 @@
 def sketch_group(first, h, cols, meta_ref, omegas_ref, turned_ref, running_ref):
     half = running_ref.shape[3]
     parts = []
-    for g in range(GROUP):
+    for g in range(LONG):
         s = meta_ref[0, first + g] % cols
         live = meta_ref[3, first + g].astype(jnp.float32)
         part = jnp.dot(omegas_ref[s], turned_ref[first + g, :, h * half:(h + 1) * half],
                        preferred_element_type=jnp.float32)
         parts.append(part * live)
-    for g in range(GROUP):
+    for g in range(LONG):
         running_ref[h, first + g] = running_ref[h, meta_ref[1, first + g]] + parts[g]
 
 
@@ -325,20 +325,20 @@
         sum_ref[h, 0] += pair_ref[h, 0]
 
     def first_half(i, carry):
-        sketch_group(i * GROUP, 0, cols, meta_ref, omegas_ref, turned_ref, running_ref)
+        sketch_group(i * LONG, 0, cols, meta_ref, omegas_ref, turned_ref, running_ref)
         return carry
 
     def second_half(i, carry):
-        @pl.when(i == groups - 1)
+        @pl.when(i == slots // LONG - 1)
         def _():
             send_sums(0)
 
-        sketch_group(i * GROUP, 1, cols, meta_ref, omegas_ref, turned_ref, running_ref)
-        return carry
-
-    lax.fori_loop(0, groups, first_half, 0)
+        sketch_group(i * LONG, 1, cols, meta_ref, omegas_ref, turned_ref, running_ref)
+        return carry
+
+    lax.fori_loop(0, slots // LONG, first_half, 0)
     swap(0)
-    lax.fori_loop(0, groups, second_half, 0)
+    lax.fori_loop(0, slots // LONG, second_half, 0)
     swap(1)
 
     def tile_step(i, carry):

time: 51.7 us -> 51.9 us (level)
  no operation moved by 1% of the time
where the time goes in v7:
time: 51.9 us; the launch traced here: 51.7 us
  Pallas kernels  51.1 us (98%)
  between operations  0.64 us (1%)
    pallas_call x1, Pallas kernels, sketch_and_factor(): pl.pallas_call(functools.partial(sketch_kernel, rows, cols), out_shape=[j...  45.8 us
    pallas_call x1, Pallas kernels, project(): pl.pallas_call(functools.partial(project_kernel, cols), out_shape=[jax.Sh...  5.24 us

profile of v7, /device:TPU:1, one launch (start us, length us, event | category | flops | bytes accessed | tf_op | source)
XLA Modules:
  0.0 51.7 jit_solution(8369634990850192937)
XLA Ops:
  0.6 45.8 %sketch_and_factor.1 = (bf16[128,256,256]{2,1,0:T(8,128)(2,1)S(1)}, f32[1,64,256]{2,1,0:T(8,128)S(1)}, bf16[16,64,256]{2,1,0:T(8,128)(2,1)S(1)}, s32[8,128]{1,0:T(8,128)S(1)}) custom-call(s32[2,128]{1,0:T(2,128)} %bitcast.1, f32[1,4,256]{2,1,0:T(4,128)} %places_ref.1, bf16[1,64,256]{2,1,0:T(8,128)(2,1)} %omega_ref.1), custom_call_target="tpu_custom_call" | custom-call | tf_op jit(solution)/shard_map/sketch_and_factor/pallas_call | solution.py:411
  46.5 5.2 %project.1 = (bf16[128,64,256]{2,1,0:T(8,128)(2,1)}, f32[1,64,256]{2,1,0:T(8,128)}) custom-call(s32[8,128]{1,0:T(8,128)S(1)} %get-tuple-element.8.meta_ref, bf16[16,64,256]{2,1,0:T(8,128)(2,1)S(1)} %get-tuple-element.9.basis_all_ref, f32[1,64,256]{2,1,0:T(8,128)S(1)} %get-tuple-element.10.basis_ref, bf16[128,256,256]{2,1,0:T(8,128)(2,1)S(1)} %get-tuple-element.11.tiles_ref), custom_call_target="tpu_custom_call" | custom-call | tf_op jit(solution)/shard_map/project/pallas_call | solution.py:471
